TPU v7x, 512 devices: a whole 4x8x8 slice. The times are simulated.
512 devices in a mesh: fsdp: 64 (over y, z_hi, core), vocab: 8 (over x, z_lo).
Axes of the slice: x: 4, y: 8, z: 8 (z_hi: 4, z_lo: 2; z = z_hi * 2 + z_lo), core: 2. Of those that a mesh axis runs over, the one named last changes fastest.
Arguments:
- hidden: bfloat16 [4, 128, 8192], P(None, 'fsdp', 'vocab'), may hold values from -6 to 6
- norm_gain: float32 [8192], P('vocab'), may hold values from 0.25 to 1.75
- head: bfloat16 [8192, 32000], P('vocab', 'fsdp'), may hold values from -8 to 8
- targets: int32 [128], P('vocab'), may hold values from 0 to 31999
- scale_index: int32 [4, 128], P(None, 'vocab'), may hold values from 0 to 3
- layer_act: bfloat16 [128, 28672], P('vocab', 'fsdp'), may hold values from -6 to 6
- down_weight: bfloat16 [28672, 8192], P('fsdp', 'vocab'), may hold values from -0.03125 to 0.03125
Outputs:
- loss: float32 [], replicated
- grad_hidden: bfloat16 [4, 128, 8192], P(None, 'fsdp', 'vocab')
- grad_head: bfloat16 [8192, 32000], P('vocab', 'fsdp')
- grad_gain: float32 [8192], P('vocab')
- grad_act: bfloat16 [128, 28672], P('vocab', 'fsdp')
- grad_down: bfloat16 [28672, 8192], P('fsdp', 'vocab')
All inputs are finite; a program needn't handle non-finite values.
Results may differ from a plain program's by a relative error of at most 0.0053.
Values may be sent and summed in bfloat16 or wider, within the bound.
A program may use at most 64 MiB of HBM per device.

v0:
```python
import jax
import jax.numpy as jnp
from jax import lax
from jax.sharding import PartitionSpec as P

EPS = 1e-05


def norm_grad(scale_rows, gated, h_rows, inner, width):
    cubed = scale_rows * scale_rows * scale_rows
    return scale_rows[..., None] * gated - h_rows * (cubed * inner / width)[..., None]


def body(hidden, norm_gain, head, targets, scale_index, layer_act, down_weight):
    exits, tok_dev, width_part = hidden.shape
    width = width_part * lax.axis_size("vocab")
    vocab_part = head.shape[1]
    fsdp_index = lax.axis_index("fsdp")
    gathered = lax.all_gather(hidden, "fsdp", axis=1, tiled=True)
    tokens_all = gathered.shape[1]
    h32 = gathered.astype(jnp.float32)
    squares = lax.psum(jnp.sum(h32 * h32, axis=-1), "vocab")
    scale = lax.rsqrt(squares / width + EPS)
    normed = (h32 * scale[..., None] * norm_gain).astype(jnp.bfloat16)
    flat = normed.reshape(exits * tokens_all, width_part)
    partial_logits = jnp.dot(flat, head, preferred_element_type=jnp.float32).reshape(
        exits, tokens_all, vocab_part
    )
    logits = lax.psum_scatter(partial_logits, "vocab", scatter_dimension=1, tiled=True)
    columns = fsdp_index * vocab_part + lax.iota(jnp.int32, vocab_part)
    onehot = columns[None, None, :] == targets[None, :, None]
    local_peak = jnp.max(logits, axis=-1)
    local_target = jnp.sum(jnp.where(onehot, logits, 0.0), axis=-1)
    peak = lax.pmax(local_peak, "fsdp")
    local_total = jnp.sum(jnp.exp(logits - peak[..., None]), axis=-1)
    total, picked = lax.psum((local_total, local_target), "fsdp")
    lse = peak + jnp.log(total)
    weights = jnp.exp2((4 - scale_index).astype(jnp.float32))
    loss_part = jnp.sum(weights * (lse - picked))
    loss = lax.psum(loss_part, "vocab") / (exits * tokens_all)
    prob = jnp.exp(logits - lse[..., None])
    dlogits = (weights[..., None] * (prob - onehot.astype(jnp.float32))).astype(jnp.bfloat16)
    dlog_all = lax.all_gather(dlogits, "vocab", axis=1, tiled=True)
    dflat = dlog_all.reshape(exits * tokens_all, vocab_part)
    grad_head = lax.dot_general(
        flat, dflat, (((0,), (0,)), ((), ())), preferred_element_type=jnp.float32
    ).astype(jnp.bfloat16)
    grad_part = lax.dot_general(
        dflat, head, (((1,), (1,)), ((), ())), preferred_element_type=jnp.float32
    ).reshape(exits, tokens_all, width_part)
    scale_own = lax.dynamic_slice_in_dim(scale, fsdp_index * tok_dev, tok_dev, 1)
    h_own = hidden.astype(jnp.float32)
    grad_own = lax.psum_scatter(grad_part, "fsdp", scatter_dimension=1, tiled=True)
    gated = grad_own * norm_gain
    inner = lax.psum(jnp.sum(gated * h_own, axis=-1), "vocab")
    grad_hidden = norm_grad(scale_own, gated, h_own, inner, width).astype(jnp.bfloat16)
    gain_part = jnp.sum(grad_own * h_own * scale_own[..., None], axis=(0, 1))
    last_rows = lax.all_gather(grad_hidden[exits - 1], "fsdp", axis=0, tiled=True)
    grad_gain = lax.psum(gain_part, "fsdp")
    acts = lax.all_gather(layer_act, "vocab", axis=0, tiled=True)
    grad_down = lax.dot_general(
        acts, last_rows, (((0,), (0,)), ((), ())), preferred_element_type=jnp.float32
    ).astype(jnp.bfloat16)
    grad_act = lax.psum_scatter(
        lax.dot_general(
            last_rows, down_weight, (((1,), (1,)), ((), ())), preferred_element_type=jnp.float32
        ),
        "vocab",
        scatter_dimension=0,
        tiled=True,
    ).astype(jnp.bfloat16)
    return (loss, grad_hidden, grad_head, grad_gain, grad_act, grad_down)


def solution(mesh):
    return jax.shard_map(
        body,
        mesh=mesh,
        in_specs=(
            P(None, "fsdp", "vocab"),
            P("vocab"),
            P("vocab", "fsdp"),
            P("vocab"),
            P(None, "vocab"),
            P("vocab", "fsdp"),
            P("fsdp", "vocab"),
        ),
        out_specs=(
            P(),
            P(None, "fsdp", "vocab"),
            P("vocab", "fsdp"),
            P("vocab"),
            P("vocab", "fsdp"),
            P("fsdp", "vocab"),
        ),
        check_vma=False,
    )
```

profile of v0, /device:TPU:1, one launch (start us, length us, event | category | flops | bytes accessed | tf_op | source)
XLA Modules:
  0.0 1352.9 jit_solution(8285479212712149365)
XLA Ops:
  7.2 0.0 copy-start
  7.2 0.0 all-gather.3.cloned.1.call-start
  7.2 1.4 copy.38
  8.6 0.0 all-gather.3.cloned.1.call-update
  8.7 0.0 reduce-scatter.3.cloned.1.call-start
  8.7 92.0 %all-gather.3.cloned.1.call-done = bf16[4,128,1024]{2,0,1:T(4,128)(2,1)} async-done(((bf16[4,2,1024]{2,0,1:T(4,128)(2,1)}), bf16[4,128,1024]{2,0,1:T(4,128)(2,1)}) %all-gather.3.cloned.1.call-update) | async-done | bytes 1048592 | tf_op jit(solution)/shard_map/all_gather | solution.py:19
  100.7 1.6 fusion
  102.3 15.2 %psum.42 = f32[4,128]{1,0:T(4,128)S(1)} all-reduce(f32[4,128]{1,0:T(4,128)S(1)} %fusion), channel_id=1, replica_groups=mesh['fsdp'=64,'vocab'=8] {'vocab'}, use_global_device_ids=true, to_apply=%region_1.0 | all-reduce | flops 512 | bytes 4096 | tf_op jit(solution)/shard_map/psum | solution.py:22
  117.5 0.0 copy-done
  117.5 0.0 copy-start.6
  117.5 3.3 fusion.6
  120.8 0.0 reduce-scatter.3.cloned.1.call-update
  120.8 0.0 all-reduce.5.cloned.1.call-start
  120.9 0.0 copy-done.6
  120.9 0.1 fusion.22
  121.0 39.4 %reduce-scatter.3.cloned.1.call-done = f32[4,16,500]{2,1,0:T(8,128)} async-done(((f32[4,128,500]{2,1,0:T(8,128)}), f32[4,16,500]{2,1,0:T(8,128)}) %reduce-scatter.3.cloned.1.call-update) | async-done | bytes 128016 | tf_op jit(solution)/shard_map/reduce_scatter | solution.py:29
  160.4 1.0 reduce_max.9
  161.4 143.5 %pmax.7 = f32[4,16]{1,0:T(4,128)S(1)} all-reduce(f32[4,16]{1,0:T(4,128)S(1)} %reduce_max.9), channel_id=1, replica_groups=mesh['fsdp'=64,'vocab'=8] {'fsdp'}, use_global_device_ids=true, to_apply=%region_4.5 | all-reduce | flops 64 | bytes 512 | tf_op jit(solution)/shard_map/pmax | solution.py:34
  304.8 1.1 select_reduce_fusion
  305.9 139.0 %psum.43 = f32[4,16]{1,0:T(4,128)S(1)} all-reduce(f32[4,16]{1,0:T(4,128)S(1)} %get-tuple-element.39), channel_id=1, replica_groups=mesh['fsdp'=64,'vocab'=8] {'fsdp'}, use_global_device_ids=true, to_apply=%region_6.7 | all-reduce | flops 64 | bytes 512 | tf_op jit(solution)/shard_map/psum | solution.py:36
  444.9 1.0 multiply_convert_fusion
  445.9 24.2 %all_gather.13 = bf16[4,128,500]{2,1,0:T(8,128)(2,1)S(1)} all-gather(bf16[4,16,500]{2,1,0:T(8,128)(2,1)S(1)} %multiply_convert_fusion), channel_id=1, replica_groups=mesh['fsdp'=64,'vocab'=8] {'vocab'}, dimensions={1}, use_global_device_ids=true | all-gather | bytes 576000 | tf_op jit(solution)/shard_map/all_gather | solution.py:43
  470.1 0.7 fusion.4
  470.8 2.6 copy.41
  473.5 0.0 all-reduce.5.cloned.1.call-update
  473.5 0.0 reduce-scatter.5.cloned.1.call-start
  473.6 1.4 dynamic-slice
  475.6 0.1 constant_dynamic-slice_fusion
  475.7 0.1 copy.40
  475.8 559.1 %all-reduce.5.cloned.1.call-done = f32[4,128,1024]{2,0,1:T(4,128)} async-done(((f32[4,128,1024]{2,0,1:T(4,128)}), f32[4,128,1024]{2,0,1:T(4,128)}) %all-reduce.5.cloned.1.call-update) | async-done | bytes 2097168
  1034.8 0.0 copy-done.2
  1034.8 0.9 fusion.19
  1035.7 142.8 %all-reduce.1 = (f32[4,16]{1,0:T(4,128)S(1)}, f32[1024]{0:T(1024)}) all-reduce(f32[4,16]{1,0:T(4,128)S(1)} %get-tuple-element.38, f32[1024]{0:T(1024)S(1)} %get-tuple-element.36), channel_id=1, replica_groups=mesh['fsdp'=64,'vocab'=8] {'fsdp'}, use_global_device_ids=true, to_apply=%region_8.9 | all-reduce | flops 1088 | bytes 8704 | tf_op jit(solution)/shard_map/psum | solution.py:36
  1178.5 0.6 multiply_reduce_fusion
  1179.1 0.1 copy.43
  1179.2 22.2 %all_gather.15 = bf16[128,448]{1,0:T(8,128)(2,1)S(1)} all-gather(bf16[16,448]{1,0:T(8,128)(2,1)S(1)} %copy-done.3), channel_id=1, replica_groups=mesh['fsdp'=64,'vocab'=8] {'vocab'}, dimensions={0}, use_global_device_ids=true | all-gather | bytes 129024 | tf_op jit(solution)/shard_map/all_gather | solution.py:60
  1201.4 15.3 %all-reduce.2 = (f32[]{:T(128)}, f32[4,2]{1,0:T(4,128)S(1)}) all-reduce(f32[]{:T(128)} %multiply_reduce_fusion, f32[4,2]{1,0:T(4,128)S(1)} %copy.43), channel_id=1, replica_groups=mesh['fsdp'=64,'vocab'=8] {'vocab'}, use_global_device_ids=true, to_apply=%region_10.11 | all-reduce | flops 9 | bytes 72 | tf_op jit(solution)/shard_map/psum | solution.py:40
  1216.7 0.1 fusion.21
  1216.8 0.1 copy.44
  1216.9 0.8 fusion.17
  1217.8 93.1 %all-gather = bf16[1,128,1024]{2,0,1:T(2,128)(2,1)S(1)} all-gather(bf16[1,2,1024]{2,0,1:T(2,128)(2,1)S(1)} %slice.4), channel_id=2, replica_groups=mesh['fsdp'=64,'vocab'=8] {'fsdp'}, dimensions={1}, use_global_device_ids=true | all-gather | bytes 266240 | tf_op jit(solution)/shard_map/all_gather | solution.py:58
  1310.9 2.3 fusion.11
  1313.2 0.0 reduce-scatter.5.cloned.1.call-update
  1313.2 2.1 bitcast_convert_fusion
  1315.3 0.6 copy.45
  1316.6 1.4 fusion.3
  1317.9 25.9 %reduce-scatter.5.cloned.1.call-done = f32[16,448]{1,0:T(8,128)} async-done(((f32[128,448]{1,0:T(8,128)}), f32[16,448]{1,0:T(8,128)}) %reduce-scatter.5.cloned.1.call-update) | async-done | bytes 28688 | tf_op jit(solution)/shard_map/reduce_scatter | solution.py:64
  1343.8 1.4 convert_element_type.46
  (14 shorter events, 0.1 us)
Async XLA Ops:
  7.2 110.3 %copy-start = (bf16[1024,500]{0,1:T(8,128)(2,1)S(1)}, bf16[1024,500]{0,1:T(8,128)(2,1)}, u32[]{:S(2)}) copy-start(bf16[1024,500]{0,1:T(8,128)(2,1)} %param.9) | copy-start | bytes 3072004
  7.2 93.5 %all-gather.3.cloned.1.call-start = ((), (), s32[]{:S(2)}) async-start(), calls=%async_computation.2 | async-start | bytes 1064960 | tf_op jit(solution)/shard_map/all_gather | solution.py:19
  8.7 151.7 %reduce-scatter.3.cloned.1.call-start = ((), (), s32[]{:S(2)}) async-start(), calls=%async_computation.3 | async-start | bytes 1179648 | tf_op jit(solution)/shard_map/reduce_scatter | solution.py:29
  117.5 3.4 copy-start.5
  117.5 3.4 copy-start.6
  120.8 914.0 %all-reduce.5.cloned.1.call-start = ((), (), s32[]{:S(2)}) async-start(), calls=%async_computation.5 | async-start | bytes 4194304
  473.5 561.4 %copy-start.2 = (bf16[4,2,1024]{2,1,0:T(2,128)(2,1)S(1)}, bf16[4,2,1024]{2,1,0:T(2,128)(2,1)}, u32[]{:S(2)}) copy-start(bf16[4,2,1024]{2,1,0:T(2,128)(2,1)} %param.7) | copy-start | bytes 49156
  473.5 561.4 %copy-start.4 = (f32[1024]{0:T(1024)S(1)}, f32[1024]{0:T(1024)}, u32[]{:S(2)}) copy-start(f32[1024]{0:T(1024)} %param.8) | copy-start | bytes 12292
  473.5 705.7 %copy-start.3 = (bf16[16,448]{1,0:T(8,128)(2,1)S(1)}, bf16[16,448]{1,0:T(8,128)(2,1)}, u32[]{:S(2)}) copy-start(bf16[16,448]{1,0:T(8,128)(2,1)} %param.12) | copy-start | bytes 43012
  473.5 839.7 %copy-start.1 = (bf16[4,128,1024]{2,0,1:T(4,128)(2,1)S(1)}, bf16[4,128,1024]{2,0,1:T(4,128)(2,1)}, u32[]{:S(2)}) copy-start(bf16[4,128,1024]{2,0,1:T(4,128)(2,1)} %all-gather.3.cloned.1.call-done) | copy-start | bytes 3145732
  473.5 870.3 %reduce-scatter.5.cloned.1.call-start = ((), (), s32[]{:S(2)}) async-start(), calls=%async_computation.4 | async-start | bytes 294912 | tf_op jit(solution)/shard_map/reduce_scatter | solution.py:64
Sparse Core Ops, SparseCore 0:
  11.9 88.7 all-gather.2
  120.9 39.4 reduce-scatter.2
  473.6 561.1 all-reduce.4
  1313.3 30.4 reduce-scatter.4
where the time goes:
time: 1360 us; the launch traced here: 1350 us
  waiting for transfers between devices  716 us (53%)
  blocking collectives  595 us (44%)
  between operations  16.3 us (1%)
    unnamed x5, waiting for transfers between devices  559 us
    psum x2, blocking collectives, body(): total, picked = lax.psum((local_total, local_target), 'fsdp')  282 us
    pmax x1, blocking collectives, body(): peak = lax.pmax(local_peak, 'fsdp')  143 us
    all_gather x1, blocking collectives, body(): lax.all_gather(grad_hidden[exits - 1], 'fsdp', axis=0, tiled=True)  93.1 us
    all_gather x1, waiting for transfers between devices, body(): gathered = lax.all_gather(hidden, 'fsdp', axis=1, tiled=True)  92 us
    reduce_scatter x1, waiting for transfers between devices, body(): lax.psum_scatter(partial_logits, 'vocab', scatter_dimension=1, tiled=True)  39.4 us
  transfers between devices with their start and end apart: 4, of which 4 were waited for; matrix products, arithmetic and copies ran while one was open for 0% of the time, Pallas kernels for 0%

commit v1 on v0

v1 whole, which is shorter than its diff:
```python
import functools

import jax
import jax.numpy as jnp
from jax import lax
from jax.experimental import pallas as pl
from jax.experimental.pallas import tpu as pltpu
from jax.sharding import PartitionSpec as P

MESH = pl.DeviceIdType.MESH
EPS = 1e-05
F32 = jnp.float32
BF16 = jnp.bfloat16
EXITS = 4
OWN = 8
VP = 512


def send_all(n, me, dev, src, dst, sems):
    def one(j, _):
        p = lax.rem(me + j, n)
        pltpu.make_async_remote_copy(
            src_ref=src(p), dst_ref=dst, send_sem=sems.at[0, j], recv_sem=sems.at[1, me],
            device_id=dev(p), device_id_type=MESH,
        ).start()
        return 0

    lax.fori_loop(1, n, one, 0)


def recv_all(n, me, dev, slot, sems, then=None):
    def one(j, _):
        p = lax.rem(me + j, n)
        pltpu.make_async_remote_copy(
            src_ref=slot(p), dst_ref=slot(p), send_sem=sems.at[0, j], recv_sem=sems.at[1, p],
            device_id=dev(p), device_id_type=MESH,
        ).wait_recv()
        if then is not None:
            then(p)
        return 0

    lax.fori_loop(1, n, one, 0)


def sent_all(n, me, dev, src, sems):
    def one(j, _):
        p = lax.rem(me + j, n)
        pltpu.make_async_remote_copy(
            src_ref=src(p), dst_ref=src(p), send_sem=sems.at[0, j], recv_sem=sems.at[1, p],
            device_id=dev(p), device_id_type=MESH,
        ).wait_send()
        return 0

    lax.fori_loop(1, n, one, 0)


def split3(x):
    hi = x.astype(BF16).astype(F32)
    rest = x - hi
    mid = rest.astype(BF16).astype(F32)
    return hi, mid, rest - mid


def stack(x):
    q = x.shape[1] // 2
    return jnp.concatenate([x[:, :q], x[:, q:]], axis=0)


def kernel(
    ny, nz, nv, vc,
    hid_ref, gain_ref, head_ref, tgt_ref, si_ref, act_ref, dw_ref,
    loss_ref, gh_ref, ghead_ref, ggain_ref, gact_ref, gdown_ref,
    hown, ga1, ga2, act, headp, hr, hg, ssum, lg, rb, st1, st2, df, rowv,
    po, pm, rc, d1, d2, rd1, rd2, d1b, d2b, rd1b, rd2b, ghs, erow, e1, gg1, gg2, lry, lr, fp, rf,
    s_act, s_a1, s_a2, s_a3, s_a4, s_c1, s_c2, s_b, s_s1, s_s2, s_c, s_dc, s_d1, s_d2, s_d3, s_d4,
    s_e1, s_g1, s_e2, s_g2, s_ec, s_f,
):
    width_part = hid_ref.shape[2]
    width = width_part * nv
    half, q = width_part // 2, width_part // 4
    ng = 2 * nz
    rv = OWN * ng
    rh = rv // 2
    rows = rv * ny
    tb = rv // EXITS
    ff = dw_ref.shape[0]

    f = lax.axis_index("fsdp")
    v = lax.axis_index("vocab")
    y = f // ng
    g = f % ng
    z = g // 2
    c = g % 2
    o = 1 - c
    dev_y = lambda p: (p * ng + g, v)
    dev_g = lambda p: (y * ng + p, v)
    dev_z = lambda p: (y * ng + p * 2 + c, v)
    dev_v = lambda p: (f, p)
    dev_c = (y * ng + z * 2 + o, v)

    def to_core(src, dst, ss, rs):
        return pltpu.make_async_remote_copy(
            src_ref=src, dst_ref=dst, send_sem=ss, recv_sem=rs, device_id=dev_c, device_id_type=MESH
        )

    barrier = pltpu.get_barrier_semaphore()

    def greet(n, me, dev):
        def one(j, _):
            pl.semaphore_signal(barrier, inc=1, device_id=dev(lax.rem(me + j, n)), device_id_type=MESH)
            return 0

        lax.fori_loop(1, n, one, 0)

    greet(ny, y, dev_y)
    greet(ng, g, dev_g)
    greet(nv, v, dev_v)

    for e in range(EXITS):
        hown[2 * e : 2 * e + 2, :] = hid_ref[e].astype(F32)
    ga1[c, y, z] = stack(hown[:, :half]).astype(BF16)
    ga2[c, z, y] = stack(hown[:, half:]).astype(BF16)
    act[v, :, :ff] = act_ref[...]
    act[v, :, ff:] = jnp.zeros((act.shape[1], act.shape[2] - ff), BF16)

    pl.semaphore_wait(barrier, ny + ng + nv - 3)

    send_all(nz, z, dev_z, lambda p: ga1.at[c, y, z], ga1.at[c, y, z], s_a1)
    send_all(ny, y, dev_y, lambda p: ga2.at[c, z, y], ga2.at[c, z, y], s_a2)
    recv_all(nz, z, dev_z, lambda p: ga1.at[c, y, p], s_a1)
    send_all(ny, y, dev_y, lambda p: ga1.at[c, y], ga1.at[c, y], s_a3)
    to_core(ga1.at[c, y], ga1.at[c, y], s_c1.at[0, y], s_c1.at[1, y]).start()
    recv_all(ny, y, dev_y, lambda p: ga2.at[c, z, p], s_a2)
    send_all(nz, z, dev_z, lambda p: ga2.at[c, z], ga2.at[c, z], s_a4)
    to_core(ga2.at[c, z], ga2.at[c, z], s_c2.at[0, z], s_c2.at[1, z]).start()
    send_all(nv, v, dev_v, lambda p: act.at[v], act.at[v], s_act)

    cut = vc // 16 * 16
    headp[:cut, :] = head_ref[:cut, :]
    tail = head_ref[cut:vc, :].astype(F32)
    headp[cut:, :] = jnp.concatenate([tail, jnp.zeros((VP - vc, width_part), F32)], axis=0).astype(BF16)

    def forward1(p):
        to_core(ga1.at[c, p], ga1.at[c, p], s_c1.at[0, p], s_c1.at[1, p]).start()

    def forward2(p):
        to_core(ga2.at[c, p], ga2.at[c, p], s_c2.at[0, p], s_c2.at[1, p]).start()

    recv_all(ny, y, dev_y, lambda p: ga1.at[c, p], s_a3, forward1)
    recv_all(nz, z, dev_z, lambda p: ga2.at[c, p], s_a4, forward2)

    def core_in1(p, _):
        to_core(ga1.at[o, p], ga1.at[o, p], s_c1.at[0, p], s_c1.at[1, p]).wait_recv()
        return 0

    def core_in2(p, _):
        to_core(ga2.at[o, p], ga2.at[o, p], s_c2.at[0, p], s_c2.at[1, p]).wait_recv()
        return 0

    lax.fori_loop(0, ny, core_in1, 0)
    lax.fori_loop(0, nz, core_in2, 0)

    def arrange(k, _):
        for cc in range(2):
            for zz in range(0, nz, 2):
                at = pl.ds(pl.multiple_of(k * rv + cc * rh + zz * OWN, 16), 16)
                squares = None
                for h in range(2):
                    a = (ga1[cc, k, zz] if h == 0 else ga2[cc, zz, k]).astype(F32)
                    b = (ga1[cc, k, zz + 1] if h == 0 else ga2[cc, zz + 1, k]).astype(F32)
                    for s in range(2):
                        x = jnp.concatenate([a[s * 8 : s * 8 + 8], b[s * 8 : s * 8 + 8]], axis=0)
                        to = slice((2 * h + s) * q, (2 * h + s + 1) * q)
                        hr[at, to] = x.astype(BF16)
                        hg[at, to] = (x * gain_ref[:, to]).astype(BF16)
                        squares = x * x if squares is None else squares + x * x
                ssum[at, :] = jnp.broadcast_to(jnp.sum(squares, axis=1, keepdims=True), (16, 128))
        return 0

    lax.fori_loop(0, ny, arrange, 0)

    lanes = lax.broadcasted_iota(jnp.int32, (rv, VP), 1)
    mt = min(rows, 256)
    for m in range(0, rows, mt):
        part = lax.dot_general(
            hg[m : m + mt, :], headp[...], (((1,), (1,)), ((), ())), preferred_element_type=F32
        )
        for k in range(mt // rv):
            piece = part[k * rv : (k + 1) * rv]
            own = ssum[m + k * rv : m + (k + 1) * rv, 0:1]
            lg[m // rv + k] = jnp.where(lanes == vc, own, piece)

    send_all(nv, v, dev_v, lambda p: lg.at[p], rb.at[v], s_b)
    rb[v] = lg[v]
    r_id = lax.broadcasted_iota(jnp.int32, (rv, 1), 0)
    exit_id = (r_id & 7) >> 1
    tok_id = (((r_id & (rh - 1)) >> 3) << 2) + ((r_id // rh) << 1) + (r_id & 1)
    l16 = lax.broadcasted_iota(jnp.int32, (rv, tb), 1)
    here = l16 == tok_id
    tgt = jnp.sum(jnp.where(here, tgt_ref[...].astype(F32), 0.0), axis=1, keepdims=True)
    index = jnp.zeros((rv, 1), F32)
    for e in range(EXITS):
        index += jnp.sum(
            jnp.where(here & (exit_id == e), si_ref[e : e + 1, :].astype(F32), 0.0), axis=1, keepdims=True
        )
    weight = jnp.exp2(4.0 - index)
    column = (lanes + f * vc).astype(F32)
    valid = lanes < vc
    onehot = (column == tgt) & valid
    recv_all(nv, v, dev_v, lambda p: rb.at[p], s_b)
    logits = rb[0]
    for p in range(1, nv):
        logits = logits + rb[p]
    scale = lax.rsqrt(logits[:, vc : vc + 1] / width + EPS)
    logits = logits * scale
    peak = jnp.max(jnp.where(valid, logits, -3e38), axis=1, keepdims=True)
    grown = jnp.where(valid, jnp.exp(jnp.minimum(logits - peak, 0.0)), 0.0)
    total = jnp.sum(grown, axis=1, keepdims=True)
    moment = jnp.sum(grown * jnp.where(valid, logits, 0.0), axis=1, keepdims=True)
    picked = jnp.sum(jnp.where(onehot, logits, 0.0), axis=1, keepdims=True)

    eye = lax.broadcasted_iota(jnp.int32, (rv, 128), 0) == lax.broadcasted_iota(jnp.int32, (rv, 128), 1)
    to_row = lambda x: jnp.sum(jnp.where(eye, x, 0.0), axis=0, keepdims=True)
    to_col = lambda x: jnp.sum(jnp.where(eye, x, 0.0), axis=1, keepdims=True)

    def put(ref, at, values):
        for i, value in enumerate(values):
            ref[at, i : i + 1, :] = value
        ref[at, len(values) :, :] = jnp.zeros((8 - len(values), 128), F32)

    def merge(ref, n):
        top = ref[0, 0:1, :]
        for p in range(1, n):
            top = jnp.maximum(top, ref[p, 0:1, :])
        tot = mom = pick = jnp.zeros((1, 128), F32)
        for p in range(n):
            by = jnp.exp(ref[p, 0:1, :] - top)
            tot = tot + by * ref[p, 1:2, :]
            mom = mom + by * ref[p, 2:3, :]
            pick = pick + ref[p, 3:4, :]
        return top, tot, mom, pick

    put(st1, g, [to_row(peak), to_row(total), to_row(moment), to_row(picked)])
    send_all(ng, g, dev_g, lambda p: st1.at[g], st1.at[g], s_s1)
    recv_all(ng, g, dev_g, lambda p: st1.at[p], s_s1)
    put(st2, y, merge(st1, ng))
    send_all(ny, y, dev_y, lambda p: st2.at[y], st2.at[y], s_s2)
    recv_all(ny, y, dev_y, lambda p: st2.at[p], s_s2)
    top, tot, mom, pick = merge(st2, ny)
    lse = to_col(top + jnp.log(tot))
    picked = to_col(pick)
    inner = weight * (to_col(mom / tot) - picked)
    dlog = weight * (jnp.exp(jnp.minimum(logits - lse, 0.0)) - onehot.astype(F32))
    out = jnp.where(valid, dlog, 0.0)
    for i, value in enumerate(split3(scale) + split3(inner) + split3(weight * (lse - picked))):
        out = jnp.where(lanes == vc + i, value, out)
    mine = pl.ds(pl.multiple_of(v * rv, rv), rv)
    df[mine, :] = out.astype(BF16)

    at_v = lambda p: df.at[pl.ds(pl.multiple_of(p * rv, rv), rv)]
    send_all(nv, v, dev_v, lambda p: at_v(v), at_v(v), s_c)
    recv_all(nv, v, dev_v, at_v, s_c)

    def rows_of(core):
        lhs = jnp.concatenate(
            [df[pl.ds(pl.multiple_of(k * rv + core * rh, rh), rh), :] for k in range(ny)], axis=0
        )
        return lax.dot_general(lhs, headp[...], (((1,), (0,)), ((), ())), preferred_element_type=F32)

    po[...] = rows_of(o).reshape(ny, rh, width_part)
    core_d = to_core(po, rc, s_dc.at[0], s_dc.at[1])
    core_d.start()
    pm[...] = rows_of(c).reshape(ny, rh, width_part)
    extra = df[:, vc - vc % 128 :].astype(F32)
    i0 = vc % 128
    pull = lambda i: extra[:, i0 + i : i0 + i + 1] + extra[:, i0 + i + 1 : i0 + i + 2] + extra[:, i0 + i + 2 : i0 + i + 3]
    scale_all = pull(0)
    rowv[:, 0:1] = scale_all
    rowv[:, 1:2] = pull(3)
    loss_ref[...] = jnp.sum(pull(6), axis=0, keepdims=True) / rows
    core_d.wait_recv()

    def pack1(k, _):
        both = pm[k] + rc[k]
        pm[k] = both
        d1[k] = both[:, :half].astype(BF16)
        return 0

    lax.fori_loop(0, ny, pack1, 0)
    send_all(ny, y, dev_y, lambda p: d1.at[p], rd1.at[y], s_d1)
    rd1[y] = d1[y]

    def pack2(k, _):
        for zz in range(nz):
            pair = jnp.concatenate(
                [pm[2 * k, zz * 8 : zz * 8 + 8, half:], pm[2 * k + 1, zz * 8 : zz * 8 + 8, half:]], axis=0
            )
            d2[zz, pl.ds(pl.multiple_of(k * 16, 16), 16), :] = pair.astype(BF16)
        return 0

    lax.fori_loop(0, ny // 2, pack2, 0)
    send_all(nz, z, dev_z, lambda p: d2.at[p], rd2.at[z], s_d2)
    rd2[z] = d2[z]

    def norm(k, _):
        at = pl.ds(pl.multiple_of(k * rv, rv), rv)
        hg[at, :] = (hr[at, :].astype(F32) * rowv[at, 0:1] * gain_ref[...]).astype(BF16)
        return 0

    lax.fori_loop(0, ny, norm, 0)
    wt = min(width_part, 256)
    for m in range(0, width_part, wt):
        part = lax.dot_general(
            df[...], hg[:, m : m + wt], (((0,), (0,)), ((), ())), preferred_element_type=F32
        )
        ghead_ref[:, m : m + wt] = part[:vc].astype(BF16)

    recv_all(ny, y, dev_y, lambda p: rd1.at[p], s_d1)
    sum1 = rd1[0].astype(F32)
    for p in range(1, ny):
        sum1 = sum1 + rd1[p].astype(F32)
    for zz in range(nz):
        d1b[zz] = stack(sum1[zz * 8 : zz * 8 + 8]).astype(BF16)
    send_all(nz, z, dev_z, lambda p: d1b.at[p], rd1b.at[z], s_d3)
    rd1b[z] = d1b[z]
    recv_all(nz, z, dev_z, lambda p: rd2.at[p], s_d2)
    sum2 = rd2[0].astype(F32)
    for p in range(1, nz):
        sum2 = sum2 + rd2[p].astype(F32)
    for k in range(ny):
        d2b[k] = stack(sum2[k * 8 : k * 8 + 8]).astype(BF16)
    send_all(ny, y, dev_y, lambda p: d2b.at[p], rd2b.at[y], s_d4)
    rd2b[y] = d2b[y]
    recv_all(nz, z, dev_z, lambda p: rd1b.at[p], s_d3)
    g1 = rd1b[0].astype(F32)
    for p in range(1, nz):
        g1 = g1 + rd1b[p].astype(F32)
    recv_all(ny, y, dev_y, lambda p: rd2b.at[p], s_d4)
    g2 = rd2b[0].astype(F32)
    for p in range(1, ny):
        g2 = g2 + rd2b[p].astype(F32)
    grad_own = jnp.concatenate([g1[:8], g1[8:], g2[:8], g2[8:]], axis=1)

    own_at = pl.ds(pl.multiple_of(y * rv + c * rh + z * 8, 8), 8)
    scale_own = rowv[own_at, 0:1]
    inner_own = rowv[own_at, 1:2]
    h_own = hown[...]
    grad_hid = scale_own * (grad_own * gain_ref[...]) - h_own * (scale_own * scale_own * inner_own / width)
    ghs[...] = grad_hid
    wk = width_part // 8
    for k in range(8):
        erow[2 * k : 2 * k + 2, :] = ghs[6:8, k * wk : (k + 1) * wk]
    e1[g] = erow[...].astype(BF16)
    send_all(ng, g, dev_g, lambda p: e1.at[g], e1.at[g], s_e1)
    gain_part = jnp.sum(grad_own * h_own * scale_own, axis=0, keepdims=True)
    for k in range(8):
        gg1[g, k : k + 1, :] = gain_part[:, k * wk : (k + 1) * wk]
    send_all(ng, g, dev_g, lambda p: gg1.at[g], gg1.at[g], s_g1)
    for e in range(EXITS):
        gh_ref[e] = ghs[2 * e : 2 * e + 2, :].astype(BF16)

    recv_all(ng, g, dev_g, lambda p: e1.at[p], s_e1)
    for p in range(ng):
        block = e1[p].astype(F32)
        for k in range(8):
            lry[2 * p : 2 * p + 2, k * wk : (k + 1) * wk] = block[2 * k : 2 * k + 2]
    lr[y] = lry[...].astype(BF16)
    half_of = lambda p, core: lr.at[p, :, pl.ds(pl.multiple_of(core * half, half), half)]
    send_all(ny, y, dev_y, lambda p: half_of(y, c), half_of(y, c), s_e2)
    recv_all(ng, g, dev_g, lambda p: gg1.at[p], s_g1)
    gain_y = gg1[0]
    for p in range(1, ng):
        gain_y = gain_y + gg1[p]
    gg2[y] = gain_y
    send_all(ny, y, dev_y, lambda p: gg2.at[y], gg2.at[y], s_g2)

    def forward_e(p):
        to_core(half_of(p, c), half_of(p, c), s_ec.at[0, p], s_ec.at[1, p]).start()

    recv_all(ny, y, dev_y, lambda p: half_of(p, c), s_e2, forward_e)
    recv_all(nv, v, dev_v, lambda p: act.at[p], s_act)

    def core_in_e(j, _):
        p = lax.rem(y + j, ny)
        to_core(half_of(p, o), half_of(p, o), s_ec.at[0, p], s_ec.at[1, p]).wait_recv()
        return 0

    lax.fori_loop(1, ny, core_in_e, 0)
    tokens = ny * lr.shape[1]
    last = lr[...].reshape(tokens, width_part)
    part = lax.dot_general(last, dw_ref[...], (((1,), (1,)), ((), ())), preferred_element_type=F32)
    tv = tokens // nv
    for p in range(nv):
        fp[p] = part[p * tv : (p + 1) * tv]
    send_all(nv, v, dev_v, lambda p: fp.at[p], rf.at[v], s_f)
    rf[v] = fp[v]
    acts = act[...].reshape(tokens, act.shape[2])
    down = lax.dot_general(acts, last, (((0,), (0,)), ((), ())), preferred_element_type=F32)
    gdown_ref[...] = down[:ff].astype(BF16)
    recv_all(ny, y, dev_y, lambda p: gg2.at[p], s_g2)
    gain_all = gg2[0]
    for p in range(1, ny):
        gain_all = gain_all + gg2[p]
    for k in range(8):
        ggain_ref[:, k * wk : (k + 1) * wk] = gain_all[k : k + 1, :]
    recv_all(nv, v, dev_v, lambda p: rf.at[p], s_f)
    acc = rf[0]
    for p in range(1, nv):
        acc = acc + rf[p]
    gact_ref[...] = acc.astype(BF16)

    sent_all(nz, z, dev_z, lambda p: ga1.at[c, y, z], s_a1)
    sent_all(ny, y, dev_y, lambda p: ga2.at[c, z, y], s_a2)
    sent_all(ny, y, dev_y, lambda p: ga1.at[c, y], s_a3)
    sent_all(nz, z, dev_z, lambda p: ga2.at[c, z], s_a4)
    sent_all(nv, v, dev_v, lambda p: act.at[v], s_act)

    def core_out1(p, _):
        to_core(ga1.at[c, p], ga1.at[c, p], s_c1.at[0, p], s_c1.at[1, p]).wait_send()
        return 0

    def core_out2(p, _):
        to_core(ga2.at[c, p], ga2.at[c, p], s_c2.at[0, p], s_c2.at[1, p]).wait_send()
        return 0

    def core_out_e(j, _):
        p = lax.rem(y + j, ny)
        to_core(half_of(p, c), half_of(p, c), s_ec.at[0, p], s_ec.at[1, p]).wait_send()
        return 0

    lax.fori_loop(0, ny, core_out1, 0)
    lax.fori_loop(0, nz, core_out2, 0)
    lax.fori_loop(1, ny, core_out_e, 0)
    sent_all(nv, v, dev_v, lambda p: lg.at[p], s_b)
    sent_all(ng, g, dev_g, lambda p: st1.at[g], s_s1)
    sent_all(ny, y, dev_y, lambda p: st2.at[y], s_s2)
    sent_all(nv, v, dev_v, lambda p: at_v(v), s_c)
    core_d.wait_send()
    sent_all(ny, y, dev_y, lambda p: d1.at[p], s_d1)
    sent_all(nz, z, dev_z, lambda p: d2.at[p], s_d2)
    sent_all(nz, z, dev_z, lambda p: d1b.at[p], s_d3)
    sent_all(ny, y, dev_y, lambda p: d2b.at[p], s_d4)
    sent_all(ng, g, dev_g, lambda p: e1.at[g], s_e1)
    sent_all(ng, g, dev_g, lambda p: gg1.at[g], s_g1)
    sent_all(ny, y, dev_y, lambda p: half_of(y, c), s_e2)
    sent_all(ny, y, dev_y, lambda p: gg2.at[y], s_g2)
    sent_all(nv, v, dev_v, lambda p: fp.at[p], s_f)


def body(ny, nz, hidden, norm_gain, head, targets, scale_index, layer_act, down_weight):
    nv = lax.axis_size("vocab")
    exits, own_tokens, w = hidden.shape
    vc = head.shape[1]
    tok_v, ff = layer_act.shape
    fpad = -(-ff // 128) * 128
    ng = 2 * nz
    rv = OWN * ng
    rh = rv // 2
    rows = rv * ny
    half, q, wk = w // 2, w // 4, w // 8
    tok_y = own_tokens * ng
    vm = pltpu.VMEM
    dma = lambda n: pltpu.SemaphoreType.DMA((2, n))
    scratch = [
        vm((OWN, w), F32), vm((2, ny, nz, 16, q), BF16), vm((2, nz, ny, 16, q), BF16),
        vm((nv, tok_v, fpad), BF16), vm((VP, w), BF16), vm((rows, w), BF16), vm((rows, w), BF16),
        vm((rows, 128), F32), vm((nv, rv, VP), F32), vm((nv, rv, VP), F32),
        vm((ng, 8, 128), F32), vm((ny, 8, 128), F32), vm((rows, VP), BF16), vm((rows, 128), F32),
        vm((ny, rh, w), F32), vm((ny, rh, w), F32), vm((ny, rh, w), F32),
        vm((ny, rh, half), BF16), vm((nz, ny * 8, half), BF16),
        vm((ny, rh, half), BF16), vm((nz, ny * 8, half), BF16),
        vm((nz, 16, q), BF16), vm((ny, 16, q), BF16), vm((nz, 16, q), BF16), vm((ny, 16, q), BF16),
        vm((OWN, w), F32), vm((16, wk), F32), vm((ng, 16, wk), BF16),
        vm((ng, 8, wk), F32), vm((ny, 8, wk), F32),
        vm((tok_y, w), F32), vm((ny, tok_y, w), BF16),
        vm((nv, tok_v, ff), F32), vm((nv, tok_v, ff), F32),
        dma(nv), dma(nz), dma(ny), dma(ny), dma(nz), dma(ny), dma(nz), dma(nv), dma(ng), dma(ny), dma(nv),
        pltpu.SemaphoreType.DMA((2,)), dma(ny), dma(nz), dma(nz), dma(ny),
        dma(ng), dma(ng), dma(ny), dma(ny), dma(ny), dma(nv),
    ]
    spec = pl.BlockSpec(memory_space=vm)
    sds = jax.ShapeDtypeStruct
    loss, grad_hidden, grad_head, grad_gain, grad_act, grad_down = pl.pallas_call(
        functools.partial(kernel, ny, nz, nv, vc),
        out_shape=(
            sds((1, 1), F32), sds(hidden.shape, BF16), sds((vc, w), BF16), sds((1, w), F32),
            sds(layer_act.shape, BF16), sds(down_weight.shape, BF16),
        ),
        in_specs=[spec] * 7,
        out_specs=(spec,) * 6,
        scratch_shapes=scratch,
        compiler_params=pltpu.CompilerParams(
            collective_id=0, has_side_effects=True, vmem_limit_bytes=56 * 1024 * 1024
        ),
    )(
        hidden, norm_gain.reshape(1, w), head.T, targets.reshape(1, -1), scale_index, layer_act, down_weight
    )
    return loss[0, 0], grad_hidden, grad_head.T, grad_gain.reshape(w), grad_act, grad_down


def solution(mesh, ny=8, nz=4):
    return jax.shard_map(
        functools.partial(body, ny, nz),
        mesh=mesh,
        in_specs=(
            P(None, "fsdp", "vocab"),
            P("vocab"),
            P("vocab", "fsdp"),
            P("vocab"),
            P(None, "vocab"),
            P("vocab", "fsdp"),
            P("fsdp", "vocab"),
        ),
        out_specs=(
            P(),
            P(None, "fsdp", "vocab"),
            P("vocab", "fsdp"),
            P("vocab"),
            P("vocab", "fsdp"),
            P("fsdp", "vocab"),
        ),
        check_vma=False,
    )
```

time: 1360 us -> 111 us (0.08)
  waiting for transfers between devices: 716 us -> 0 us
  blocking collectives: 595 us -> 0 us
  Pallas kernels: 0 us -> 103 us
  between operations: 16.3 us -> 2.36 us
    unnamed x5 -> x0, waiting for transfers between devices: 559 us -> none
    psum x4 -> x0, blocking collectives: 312 us -> none  [the longest x2 282 us: body(): total, picked = lax.psum((local_total, local_target), 'fsdp')]
    pmax x1 -> x0, blocking collectives: 143 us -> none  [body(): peak = lax.pmax(local_peak, 'fsdp')]
    all_gather x3 -> x0, blocking collectives: 140 us -> none  [the longest x1 93.1 us: body(): lax.all_gather(grad_hidden[exits - 1], 'fsdp', axis=0, tiled=True)]
    pallas_call x0 -> x1, Pallas kernels: none -> 103 us  [body(): pl.pallas_call(functools.partial(kernel, ny, nz, nv, vc), out_shape=(sds(...]
    all_gather x1 -> x0, waiting for transfers between devices: 92 us -> none  [body(): gathered = lax.all_gather(hidden, 'fsdp', axis=1, tiled=True)]
    reduce_scatter x2 -> x0, waiting for transfers between devices: 65.3 us -> none  [the longest x1 39.4 us: body(): lax.psum_scatter(partial_logits, 'vocab', scatter_dimension=1, tiled=True)]
  transfers between devices with their start and end apart: 4 -> 0, of which waited for: 4 -> 0; matrix products, arithmetic and copies ran while one was open for 0% -> 0% of each run, Pallas kernels for 0% -> 0%
where the time goes in v1:
time: 111 us
  Pallas kernels  103 us (93%)
  local copies, waits for them, and re-layouts  5.2 us (5%)
  between operations  2.36 us (2%)
    pallas_call x1, Pallas kernels, body(): pl.pallas_call(functools.partial(kernel, ny, nz, nv, vc), out_shape=(sds(...  103 us
    unnamed x13, local copies, waits for them, and re-layouts  5.2 us

profile of v1, /device:TPU:1, one launch (start us, length us, event | category | flops | bytes accessed | tf_op | source)
XLA Modules:
  0.0 110.9 jit_solution(8230906122626158411)
XLA Ops:
  0.6 103.3 %shard_map.118 = (f32[1,1]{1,0:T(1,128)}, bf16[4,2,1024]{2,1,0:T(2,128)(2,1)}, bf16[500,1024]{1,0:T(8,128)(2,1)}, f32[1,1024]{1,0:T(1,128)}, bf16[16,448]{1,0:T(8,128)(2,1)}, /*index=5*/bf16[448,1024]{1,0:T(8,128)(2,1)}) custom-call(bf16[4,2,1024]{2,1,0:T(2,128)(2,1)} %hid_ref.1, f32[1,1024]{1,0:T(1,128)} %bitcast.9, bf16[500,1024]{1,0:T(8,128)(2,1)} %bitcast.6, ...), custom_call_target="tpu_custom_call" | custom-call | tf_op jit(solution)/shard_map/pallas_call | solution.py:483
  103.9 0.0 copy-start.2
  104.5 0.1 copy-done.2
  104.7 0.6 copy.20
  105.3 0.0 copy-start.3
  105.3 0.0 copy-start.1
  105.3 0.0 copy-start
  105.3 2.3 %copy.21 = bf16[1024,500]{0,1:T(8,128)(2,1)} copy(bf16[1024,500]{0,1:T(8,128)(2,1)} %bitcast.7) | data formatting | bytes 2048000
  107.6 0.0 copy-done.3
  107.6 0.6 copy.22
  108.2 0.0 copy-done.1
  108.2 0.6 copy.23
  108.8 0.0 copy-done
  108.8 0.9 copy.24
Async XLA Ops:
  103.9 0.7 copy-start.2
  105.3 2.3 %copy-start.3 = (f32[1,1024]{1,0:T(1,128)S(1)}, f32[1,1024]{1,0:T(1,128)}, u32[]{:S(2)}) copy-start(f32[1,1024]{1,0:T(1,128)} %get-tuple-element.15) | copy-start | bytes 12292
  105.3 2.9 %copy-start.1 = (bf16[16,448]{1,0:T(8,128)(2,1)S(1)}, bf16[16,448]{1,0:T(8,128)(2,1)}, u32[]{:S(2)}) copy-start(bf16[16,448]{1,0:T(8,128)(2,1)} %get-tuple-element.28) | copy-start | bytes 43012
  105.3 3.5 %copy-start = (bf16[448,1024]{1,0:T(8,128)(2,1)S(1)}, bf16[448,1024]{1,0:T(8,128)(2,1)}, u32[]{:S(2)}) copy-start(bf16[448,1024]{1,0:T(8,128)(2,1)} %get-tuple-element.29) | copy-start | bytes 2752516

commit v2 on v1

v2 whole, which is shorter than its diff:
```python
import functools

import jax
import jax.numpy as jnp
from jax import lax
from jax.experimental import pallas as pl
from jax.experimental.pallas import tpu as pltpu
from jax.sharding import PartitionSpec as P

MESH = pl.DeviceIdType.MESH
EPS = 1e-05
F32 = jnp.float32
BF16 = jnp.bfloat16
EXITS = 4
OWN = 8
VP = 512


class Exchange:
    def __init__(self, n, me, dev, src, slot, sems):
        self.n, self.me, self.dev, self.src, self.slot, self.sems = n, me, dev, src, slot, sems

    def copy(self, p, j, src, dst, recv):
        return pltpu.make_async_remote_copy(
            src_ref=src, dst_ref=dst, send_sem=self.sems.at[0, j], recv_sem=self.sems.at[1, recv],
            device_id=self.dev(p), device_id_type=MESH,
        )

    def each(self, do):
        def one(j, _):
            do(lax.rem(self.me + j, self.n), j)
            return 0

        lax.fori_loop(1, self.n, one, 0)

    def start(self):
        self.each(lambda p, j: self.copy(p, j, self.src(p), self.slot(self.me), self.me).start())
        return self

    def recv(self, then=None):
        def one(p, j):
            self.copy(p, j, self.slot(p), self.slot(p), p).wait_recv()
            if then is not None:
                then(p)

        self.each(one)

    def sent(self):
        self.each(lambda p, j: self.copy(p, j, self.src(p), self.slot(self.me), self.me).wait_send())


def split3(x):
    hi = x.astype(BF16).astype(F32)
    rest = x - hi
    mid = rest.astype(BF16).astype(F32)
    return hi, mid, rest - mid


def stack(x):
    q = x.shape[1] // 2
    return jnp.concatenate([x[:, :q], x[:, q:]], axis=0)


def kernel(
    ny, nz, nv, vc,
    hid_ref, gain_ref, head_ref, tgt_ref, si_ref, act_ref, dw_ref,
    loss_ref, gh_ref, ghead_ref, ggain_ref, gact_ref, gdown_ref,
    hown, ga, act, headv, headp, dwv, gheadv, gdownv, hr, hg, lg, rb, st1, st2, df, rowv,
    po, pm, rc, d1, d2, rd1, rd2, d1b, d2b, rd1b, rd2b, ghs, erow, e1, gg1, gg2, lry, lr, fp, rf,
    s_act, s_in, s_out, r_a, s_a0z, s_a0y, s_a1y, s_a1z, s_ac, s_b, s_s1, s_s2, s_c, s_dc, s_d1, s_d2, s_d3, s_d4,
    s_e1, s_g1, s_e2, s_g2, s_ec, s_f,
):
    width_part = hid_ref.shape[2]
    width = width_part * nv
    half, q = width_part // 2, width_part // 4
    ng = 2 * nz
    rv = OWN * ng
    rh = rv // 2
    rows = rv * ny
    tb = rv // EXITS
    ff = dw_ref.shape[0]

    f = lax.axis_index("fsdp")
    v = lax.axis_index("vocab")
    y = f // ng
    g = f % ng
    z = g // 2
    c = g % 2
    o = 1 - c
    dev_y = lambda p: (p * ng + g, v)
    dev_g = lambda p: (y * ng + p, v)
    dev_z = lambda p: (y * ng + p * 2 + c, v)
    dev_v = lambda p: (f, p)
    dev_c = (y * ng + z * 2 + o, v)

    def to_core(src, dst, ss, rs):
        return pltpu.make_async_remote_copy(
            src_ref=src, dst_ref=dst, send_sem=ss, recv_sem=rs, device_id=dev_c, device_id_type=MESH
        )

    barrier = pltpu.get_barrier_semaphore()

    def greet(n, me, dev):
        def one(j, _):
            pl.semaphore_signal(barrier, inc=1, device_id=dev(lax.rem(me + j, n)), device_id_type=MESH)
            return 0

        lax.fori_loop(1, n, one, 0)

    load_head = pltpu.make_async_copy(head_ref, headv, s_in.at[0])
    load_down = pltpu.make_async_copy(dw_ref, dwv, s_in.at[1])
    greet(ny, y, dev_y)
    greet(ng, g, dev_g)
    greet(nv, v, dev_v)
    load_head.start()
    load_down.start()

    for e in range(EXITS):
        hown[2 * e : 2 * e + 2, :] = hid_ref[e].astype(F32)
    ga[c, y, z, 0] = stack(hown[:, :half]).astype(BF16)
    ga[c, y, z, 1] = stack(hown[:, half:]).astype(BF16)
    act[v, :, :ff] = act_ref[...]
    act[v, :, ff:] = jnp.zeros((act.shape[1], act.shape[2] - ff), BF16)

    pl.semaphore_wait(barrier, ny + ng + nv - 3)

    half_of = lambda p, core: lr.at[p, :, pl.ds(pl.multiple_of(core * half, half), half)]
    at_v = lambda p: df.at[pl.ds(pl.multiple_of(p * rv, rv), rv)]
    in_y = functools.partial(Exchange, ny, y, dev_y)
    in_z = functools.partial(Exchange, nz, z, dev_z)
    in_g = functools.partial(Exchange, ng, g, dev_g)
    in_v = functools.partial(Exchange, nv, v, dev_v)
    x_act = in_v(lambda p: act.at[v], lambda p: act.at[p], s_act)
    x_b = in_v(lambda p: lg.at[p], lambda p: rb.at[p], s_b)
    x_s1 = in_g(lambda p: st1.at[g], lambda p: st1.at[p], s_s1)
    x_s2 = in_y(lambda p: st2.at[y], lambda p: st2.at[p], s_s2)
    x_c = in_v(lambda p: at_v(v), at_v, s_c)
    x_d1 = in_y(lambda p: d1.at[p], lambda p: rd1.at[p], s_d1)
    x_d2 = in_z(lambda p: d2.at[p], lambda p: rd2.at[p], s_d2)
    x_d3 = in_z(lambda p: d1b.at[p], lambda p: rd1b.at[p], s_d3)
    x_d4 = in_y(lambda p: d2b.at[p], lambda p: rd2b.at[p], s_d4)
    x_e1 = in_g(lambda p: e1.at[g], lambda p: e1.at[p], s_e1)
    x_g1 = in_g(lambda p: gg1.at[g], lambda p: gg1.at[p], s_g1)
    x_e2 = in_y(lambda p: half_of(y, c), lambda p: half_of(p, c), s_e2)
    x_g2 = in_y(lambda p: gg2.at[y], lambda p: gg2.at[p], s_g2)
    x_f = in_v(lambda p: fp.at[p], lambda p: rf.at[p], s_f)

    def block(dev, p, h, yy, zz, send):
        ref = ga.at[c, yy, zz, h]
        return pltpu.make_async_remote_copy(
            src_ref=ref, dst_ref=ref, send_sem=send, recv_sem=r_a.at[h, yy, zz],
            device_id=dev(p), device_id_type=MESH,
        )

    def each(n, me, do):
        def one(j, _):
            do(lax.rem(me + j, n), j)
            return 0

        lax.fori_loop(1, n, one, 0)

    own_z = lambda p, j: block(dev_z, p, 0, y, z, s_a0z.at[j])
    own_y = lambda p, j: block(dev_y, p, 1, y, z, s_a1y.at[j])
    on_y = lambda zz: lambda p, j: block(dev_y, p, 0, y, zz, s_a0y.at[zz, j])
    on_z = lambda yy: lambda p, j: block(dev_z, p, 1, yy, z, s_a1z.at[yy, j])
    begin = lambda make: lambda p, j: make(p, j).start()
    finish = lambda make: lambda p, j: make(p, j).wait_send()

    def arrived(h, yy, zz):
        block(dev_y, y, h, yy, zz, s_a0z.at[0]).wait_recv()

    each(nz, z, begin(own_z))
    each(ny, y, begin(own_y))
    each(ny, y, begin(on_y(z)))
    each(nz, z, begin(on_z(y)))
    x_act.start()

    load_head.wait()
    cut = vc // 16 * 16
    headp[:cut, :] = headv[:cut, :]
    tail = headv[cut:vc, :].astype(F32)
    headp[cut:, :] = jnp.concatenate([tail, jnp.zeros((VP - vc, width_part), F32)], axis=0).astype(BF16)

    for d in range(1, max(ny, nz) // 2 + 1):
        for shift in (d, -d):
            if d <= ny // 2 and (shift > 0 or 2 * d < ny):
                yy = lax.rem(y + shift + ny, ny)
                arrived(1, yy, z)
                each(nz, z, begin(on_z(yy)))
            if d <= nz // 2 and (shift > 0 or 2 * d < nz):
                zz = lax.rem(z + shift + nz, nz)
                arrived(0, y, zz)
                each(ny, y, begin(on_y(zz)))

    def across(yy):
        ref = ga.at[c, yy]
        return to_core(ref, ref, s_ac.at[0, yy], s_ac.at[1, yy])

    def nearest(j):
        return lax.rem(y + ny + jnp.where(j % 2 == 1, (j + 1) // 2, -(j // 2)), ny)

    def line_of(j, _):
        yy = nearest(j)

        @pl.when(j > 0)
        def _():
            lax.fori_loop(0, nz, lambda zz, _: (arrived(0, yy, zz), 0)[1], 0)

        each(nz, z, lambda p, _: arrived(1, yy, p))
        across(yy).start()
        return 0

    lanes = lax.broadcasted_iota(jnp.int32, (rv, VP), 1)

    def to_tokens(k):
        return pltpu.make_async_remote_copy(
            src_ref=lg.at[k], dst_ref=rb.at[v], send_sem=s_b.at[0, k], recv_sem=s_b.at[1, v],
            device_id=dev_v(k), device_id_type=MESH,
        )

    def rows_in(j):
        k = nearest(j)
        to_core(ga.at[o, k], ga.at[o, k], s_ac.at[0, k], s_ac.at[1, k]).wait_recv()
        at = pl.ds(pl.multiple_of(k * rv, rv), rv)
        sums = []
        for cc in range(2):
            for zz in range(0, nz, 2):
                to_at = pl.ds(pl.multiple_of(k * rv + cc * rh + zz * OWN, 16), 16)
                squares = None
                for h in range(2):
                    a = ga[cc, k, zz, h].astype(F32)
                    b = ga[cc, k, zz + 1, h].astype(F32)
                    for s in range(2):
                        x = jnp.concatenate([a[s * 8 : s * 8 + 8], b[s * 8 : s * 8 + 8]], axis=0)
                        to = slice((2 * h + s) * q, (2 * h + s + 1) * q)
                        hr[to_at, to] = x.astype(BF16)
                        hg[to_at, to] = (x * gain_ref[:, to]).astype(BF16)
                        squares = x * x if squares is None else squares + x * x
                sums.append(jnp.sum(squares, axis=1, keepdims=True))
        part = lax.dot_general(
            hg[at, :], headp[...], (((1,), (1,)), ((), ())), preferred_element_type=F32
        )
        lg[k] = jnp.where(lanes == vc, jnp.concatenate(sums, axis=0), part)

        @pl.when(k != v)
        def _():
            to_tokens(k).start()

        @pl.when(k == v)
        def _():
            rb[v] = lg[v]

    line_of(0, 0)

    def step(j, _):
        line_of(j, 0)
        rows_in(j - 1)
        return 0

    lax.fori_loop(1, ny, step, 0)
    rows_in(ny - 1)

    r_id = lax.broadcasted_iota(jnp.int32, (rv, 1), 0)
    exit_id = (r_id & 7) >> 1
    tok_id = (((r_id & (rh - 1)) >> 3) << 2) + ((r_id // rh) << 1) + (r_id & 1)
    l16 = lax.broadcasted_iota(jnp.int32, (rv, tb), 1)
    here = l16 == tok_id
    tgt = jnp.sum(jnp.where(here, tgt_ref[...].astype(F32), 0.0), axis=1, keepdims=True)
    index = jnp.zeros((rv, 1), F32)
    for e in range(EXITS):
        index += jnp.sum(
            jnp.where(here & (exit_id == e), si_ref[e : e + 1, :].astype(F32), 0.0), axis=1, keepdims=True
        )
    weight = jnp.exp2(4.0 - index)
    column = (lanes + f * vc).astype(F32)
    valid = lanes < vc
    onehot = (column == tgt) & valid
    x_b.recv()
    logits = rb[0]
    for p in range(1, nv):
        logits = logits + rb[p]
    scale = lax.rsqrt(logits[:, vc : vc + 1] / width + EPS)
    logits = logits * scale
    peak = jnp.max(jnp.where(valid, logits, -3e38), axis=1, keepdims=True)
    grown = jnp.where(valid, jnp.exp(jnp.minimum(logits - peak, 0.0)), 0.0)
    total = jnp.sum(grown, axis=1, keepdims=True)
    moment = jnp.sum(grown * jnp.where(valid, logits, 0.0), axis=1, keepdims=True)
    picked = jnp.sum(jnp.where(onehot, logits, 0.0), axis=1, keepdims=True)

    eye = lax.broadcasted_iota(jnp.int32, (rv, 128), 0) == lax.broadcasted_iota(jnp.int32, (rv, 128), 1)
    to_row = lambda x: jnp.sum(jnp.where(eye, x, 0.0), axis=0, keepdims=True)
    to_col = lambda x: jnp.sum(jnp.where(eye, x, 0.0), axis=1, keepdims=True)

    def put(ref, at, values):
        for i, value in enumerate(values):
            ref[at, i : i + 1, :] = value
        ref[at, len(values) :, :] = jnp.zeros((8 - len(values), 128), F32)

    def merge(ref, n):
        top = ref[0, 0:1, :]
        for p in range(1, n):
            top = jnp.maximum(top, ref[p, 0:1, :])
        tot = mom = pick = jnp.zeros((1, 128), F32)
        for p in range(n):
            by = jnp.exp(ref[p, 0:1, :] - top)
            tot = tot + by * ref[p, 1:2, :]
            mom = mom + by * ref[p, 2:3, :]
            pick = pick + ref[p, 3:4, :]
        return top, tot, mom, pick

    put(st1, g, [to_row(peak), to_row(total), to_row(moment), to_row(picked)])
    x_s1.start()
    x_s1.recv()
    put(st2, y, merge(st1, ng))
    x_s2.start()
    x_s2.recv()
    top, tot, mom, pick = merge(st2, ny)
    lse = to_col(top + jnp.log(tot))
    picked = to_col(pick)
    inner = weight * (to_col(mom / tot) - picked)
    dlog = weight * (jnp.exp(jnp.minimum(logits - lse, 0.0)) - onehot.astype(F32))
    out = jnp.where(valid, dlog, 0.0)
    for i, value in enumerate(split3(scale) + split3(inner) + split3(weight * (lse - picked))):
        out = jnp.where(lanes == vc + i, value, out)
    mine = pl.ds(pl.multiple_of(v * rv, rv), rv)
    df[mine, :] = out.astype(BF16)

    x_c.start()
    x_c.recv()

    def rows_of(core):
        lhs = jnp.concatenate(
            [df[pl.ds(pl.multiple_of(k * rv + core * rh, rh), rh), :] for k in range(ny)], axis=0
        )
        return lax.dot_general(lhs, headp[...], (((1,), (0,)), ((), ())), preferred_element_type=F32)

    po[...] = rows_of(o).reshape(ny, rh, width_part)
    core_d = to_core(po, rc, s_dc.at[0], s_dc.at[1])
    core_d.start()
    pm[...] = rows_of(c).reshape(ny, rh, width_part)
    extra = df[:, vc - vc % 128 :].astype(F32)
    i0 = vc % 128
    pull = lambda i: extra[:, i0 + i : i0 + i + 1] + extra[:, i0 + i + 1 : i0 + i + 2] + extra[:, i0 + i + 2 : i0 + i + 3]
    scale_all = pull(0)
    rowv[:, 0:1] = scale_all
    rowv[:, 1:2] = pull(3)
    loss_ref[...] = jnp.sum(pull(6), axis=0, keepdims=True) / rows
    core_d.wait_recv()

    def pack1(k, _):
        both = pm[k] + rc[k]
        pm[k] = both
        d1[k] = both[:, :half].astype(BF16)
        return 0

    lax.fori_loop(0, ny, pack1, 0)
    x_d1.start()
    rd1[y] = d1[y]

    def pack2(k, _):
        for zz in range(nz):
            pair = jnp.concatenate(
                [pm[2 * k, zz * 8 : zz * 8 + 8, half:], pm[2 * k + 1, zz * 8 : zz * 8 + 8, half:]], axis=0
            )
            d2[zz, pl.ds(pl.multiple_of(k * 16, 16), 16), :] = pair.astype(BF16)
        return 0

    lax.fori_loop(0, ny // 2, pack2, 0)
    x_d2.start()
    rd2[z] = d2[z]

    def norm(k, _):
        at = pl.ds(pl.multiple_of(k * rv, rv), rv)
        hg[at, :] = (hr[at, :].astype(F32) * rowv[at, 0:1] * gain_ref[...]).astype(BF16)
        return 0

    lax.fori_loop(0, ny, norm, 0)
    wt = min(width_part, 256)
    for m in range(0, width_part, wt):
        part = lax.dot_general(
            df[...], hg[:, m : m + wt], (((0,), (0,)), ((), ())), preferred_element_type=F32
        )
        gheadv[:, m : m + wt] = part[:vc].astype(BF16)
    store_head = pltpu.make_async_copy(gheadv, ghead_ref, s_out.at[0])
    store_head.start()

    x_d1.recv()
    sum1 = rd1[0].astype(F32)
    for p in range(1, ny):
        sum1 = sum1 + rd1[p].astype(F32)
    for zz in range(nz):
        d1b[zz] = stack(sum1[zz * 8 : zz * 8 + 8]).astype(BF16)
    x_d3.start()
    rd1b[z] = d1b[z]
    x_d2.recv()
    sum2 = rd2[0].astype(F32)
    for p in range(1, nz):
        sum2 = sum2 + rd2[p].astype(F32)
    for k in range(ny):
        d2b[k] = stack(sum2[k * 8 : k * 8 + 8]).astype(BF16)
    x_d4.start()
    rd2b[y] = d2b[y]
    x_d3.recv()
    g1 = rd1b[0].astype(F32)
    for p in range(1, nz):
        g1 = g1 + rd1b[p].astype(F32)
    x_d4.recv()
    g2 = rd2b[0].astype(F32)
    for p in range(1, ny):
        g2 = g2 + rd2b[p].astype(F32)
    grad_own = jnp.concatenate([g1[:8], g1[8:], g2[:8], g2[8:]], axis=1)

    own_at = pl.ds(pl.multiple_of(y * rv + c * rh + z * 8, 8), 8)
    scale_own = rowv[own_at, 0:1]
    inner_own = rowv[own_at, 1:2]
    h_own = hown[...]
    grad_hid = scale_own * (grad_own * gain_ref[...]) - h_own * (scale_own * scale_own * inner_own / width)
    ghs[...] = grad_hid
    wk = width_part // 8
    for k in range(8):
        erow[2 * k : 2 * k + 2, :] = ghs[6:8, k * wk : (k + 1) * wk]
    e1[g] = erow[...].astype(BF16)
    x_e1.start()
    gain_part = jnp.sum(grad_own * h_own * scale_own, axis=0, keepdims=True)
    for k in range(8):
        gg1[g, k : k + 1, :] = gain_part[:, k * wk : (k + 1) * wk]
    x_g1.start()
    for e in range(EXITS):
        gh_ref[e] = ghs[2 * e : 2 * e + 2, :].astype(BF16)

    x_e1.recv()
    for p in range(ng):
        tile = e1[p].astype(F32)
        for k in range(8):
            lry[2 * p : 2 * p + 2, k * wk : (k + 1) * wk] = tile[2 * k : 2 * k + 2]
    lr[y] = lry[...].astype(BF16)
    x_e2.start()
    x_g1.recv()
    gain_y = gg1[0]
    for p in range(1, ng):
        gain_y = gain_y + gg1[p]
    gg2[y] = gain_y
    x_g2.start()

    def forward_e(p):
        to_core(half_of(p, c), half_of(p, c), s_ec.at[0, p], s_ec.at[1, p]).start()

    x_e2.recv(forward_e)
    x_act.recv()

    def core_in_e(j, _):
        p = lax.rem(y + j, ny)
        to_core(half_of(p, o), half_of(p, o), s_ec.at[0, p], s_ec.at[1, p]).wait_recv()
        return 0

    lax.fori_loop(1, ny, core_in_e, 0)
    tokens = ny * lr.shape[1]
    last = lr[...].reshape(tokens, width_part)
    load_down.wait()
    part = lax.dot_general(last, dwv[...], (((1,), (1,)), ((), ())), preferred_element_type=F32)
    tv = tokens // nv
    for p in range(nv):
        fp[p] = part[p * tv : (p + 1) * tv]
    x_f.start()
    rf[v] = fp[v]
    acts = act[...].reshape(tokens, act.shape[2])
    down = lax.dot_general(acts, last, (((0,), (0,)), ((), ())), preferred_element_type=F32)
    gdownv[...] = down[:ff].astype(BF16)
    store_down = pltpu.make_async_copy(gdownv, gdown_ref, s_out.at[1])
    store_down.start()
    x_g2.recv()
    gain_all = gg2[0]
    for p in range(1, ny):
        gain_all = gain_all + gg2[p]
    for k in range(8):
        ggain_ref[:, k * wk : (k + 1) * wk] = gain_all[k : k + 1, :]
    x_f.recv()
    acc = rf[0]
    for p in range(1, nv):
        acc = acc + rf[p]
    gact_ref[...] = acc.astype(BF16)

    each(nz, z, finish(own_z))
    each(ny, y, finish(own_y))
    lax.fori_loop(0, nz, lambda zz, _: (each(ny, y, finish(on_y(zz))), 0)[1], 0)
    lax.fori_loop(0, ny, lambda yy, _: (each(nz, z, finish(on_z(yy))), 0)[1], 0)
    lax.fori_loop(0, ny, lambda yy, _: (across(yy).wait_send(), 0)[1], 0)
    x_act.sent()

    def core_out_e(j, _):
        p = lax.rem(y + j, ny)
        to_core(half_of(p, c), half_of(p, c), s_ec.at[0, p], s_ec.at[1, p]).wait_send()
        return 0

    lax.fori_loop(1, ny, core_out_e, 0)
    each(nv, v, lambda p, _: to_tokens(p).wait_send())
    x_s1.sent()
    x_s2.sent()
    x_c.sent()
    core_d.wait_send()
    x_d1.sent()
    x_d2.sent()
    x_d3.sent()
    x_d4.sent()
    x_e1.sent()
    x_g1.sent()
    x_e2.sent()
    x_g2.sent()
    x_f.sent()
    store_head.wait()
    store_down.wait()


def hand_on_kernel(n, *refs):
    sems = refs[2 * n]
    copies = [pltpu.make_async_copy(refs[i], refs[n + i], sems.at[i]) for i in range(n)]
    for copy in copies:
        copy.start()
    for copy in copies:
        copy.wait()


def hand_on(arrays):
    n = len(arrays)
    hbm = pl.BlockSpec(memory_space=pl.ANY)
    return pl.pallas_call(
        functools.partial(hand_on_kernel, n),
        out_shape=tuple(jax.ShapeDtypeStruct(a.shape, a.dtype) for a in arrays),
        in_specs=[hbm] * n,
        out_specs=(hbm,) * n,
        scratch_shapes=[pltpu.SemaphoreType.DMA((n,))],
        compiler_params=pltpu.CompilerParams(vmem_limit_bytes=56 * 1024 * 1024),
    )(*arrays)


def body(ny, nz, hidden, norm_gain, head, targets, scale_index, layer_act, down_weight):
    nv = lax.axis_size("vocab")
    exits, own_tokens, w = hidden.shape
    vc = head.shape[1]
    tok_v, ff = layer_act.shape
    fpad = -(-ff // 128) * 128
    ng = 2 * nz
    rv = OWN * ng
    rh = rv // 2
    rows = rv * ny
    half, q, wk = w // 2, w // 4, w // 8
    tok_y = own_tokens * ng
    vm = pltpu.VMEM
    sem = lambda *n: pltpu.SemaphoreType.DMA(n)
    dma = lambda n: sem(2, n)
    scratch = [
        vm((OWN, w), F32), vm((2, ny, nz, 2, 16, q), BF16),
        vm((nv, tok_v, fpad), BF16), vm((vc, w), BF16), vm((VP, w), BF16), vm((ff, w), BF16),
        vm((vc, w), BF16), vm((ff, w), BF16), vm((rows, w), BF16), vm((rows, w), BF16),
        vm((nv, rv, VP), F32), vm((nv, rv, VP), F32),
        vm((ng, 8, 128), F32), vm((ny, 8, 128), F32), vm((rows, VP), BF16), vm((rows, 128), F32),
        vm((ny, rh, w), F32), vm((ny, rh, w), F32), vm((ny, rh, w), F32),
        vm((ny, rh, half), BF16), vm((nz, ny * 8, half), BF16),
        vm((ny, rh, half), BF16), vm((nz, ny * 8, half), BF16),
        vm((nz, 16, q), BF16), vm((ny, 16, q), BF16), vm((nz, 16, q), BF16), vm((ny, 16, q), BF16),
        vm((OWN, w), F32), vm((16, wk), F32), vm((ng, 16, wk), BF16),
        vm((ng, 8, wk), F32), vm((ny, 8, wk), F32),
        vm((tok_y, w), F32), vm((ny, tok_y, w), BF16),
        vm((nv, tok_v, ff), F32), vm((nv, tok_v, ff), F32),
        dma(nv), sem(2), sem(2), sem(2, ny, nz), sem(nz), sem(nz, ny), sem(ny), sem(ny, nz), dma(ny),
        dma(nv), dma(ng), dma(ny), dma(nv),
        sem(2), dma(ny), dma(nz), dma(nz), dma(ny),
        dma(ng), dma(ng), dma(ny), dma(ny), dma(ny), dma(nv),
    ]
    spec = pl.BlockSpec(memory_space=vm)
    hbm = pl.BlockSpec(memory_space=pl.ANY)
    sds = jax.ShapeDtypeStruct
    results = pl.pallas_call(
        functools.partial(kernel, ny, nz, nv, vc),
        out_shape=(
            sds((1, 1), F32), sds(hidden.shape, BF16), sds((vc, w), BF16), sds((1, w), F32),
            sds(layer_act.shape, BF16), sds(down_weight.shape, BF16),
        ),
        in_specs=[spec, spec, hbm, spec, spec, spec, hbm],
        out_specs=(spec, spec, hbm, spec, spec, hbm),
        scratch_shapes=scratch,
        compiler_params=pltpu.CompilerParams(
            collective_id=0, has_side_effects=True, vmem_limit_bytes=56 * 1024 * 1024
        ),
    )(
        hidden, norm_gain.reshape(1, w), head.T, targets.reshape(1, -1), scale_index, layer_act, down_weight
    )
    loss, grad_hidden, grad_head, grad_gain, grad_act, grad_down = hand_on(results)
    return loss[0, 0], grad_hidden, grad_head.T, grad_gain.reshape(w), grad_act, grad_down


def solution(mesh, ny=8, nz=4):
    return jax.shard_map(
        functools.partial(body, ny, nz),
        mesh=mesh,
        in_specs=(
            P(None, "fsdp", "vocab"),
            P("vocab"),
            P("vocab", "fsdp"),
            P("vocab"),
            P(None, "vocab"),
            P("vocab", "fsdp"),
            P("fsdp", "vocab"),
        ),
        out_specs=(
            P(),
            P(None, "fsdp", "vocab"),
            P("vocab", "fsdp"),
            P("vocab"),
            P("vocab", "fsdp"),
            P("fsdp", "vocab"),
        ),
        check_vma=False,
    )
```

time: 111 us -> 167 us (1.50)
  Pallas kernels: 103 us -> 166 us
  local copies, waits for them, and re-layouts: 5.2 us -> 0 us
  between operations: 2.36 us -> 0.64 us
    pallas_call x0 -> x1, Pallas kernels: none -> 62 us  [hand_on(): pl.pallas_call(functools.partial(hand_on_kernel, n), out_shape=tuple((jax...]
    unnamed x13 -> x0, local copies, waits for them, and re-layouts: 5.2 us -> none
where the time goes in v2:
time: 167 us; the launch traced here: 166 us
  Pallas kernels  166 us (99%)
    pallas_call x1, Pallas kernels, body(): pl.pallas_call(functools.partial(kernel, ny, nz, nv, vc), out_shape=(sds(...  104 us
    pallas_call x1, Pallas kernels, hand_on(): pl.pallas_call(functools.partial(hand_on_kernel, n), out_shape=tuple((jax...  62 us

profile of v2, /device:TPU:1, one launch (start us, length us, event | category | flops | bytes accessed | tf_op | source)
XLA Modules:
  0.0 166.4 jit_solution(15142184366283635702)
XLA Ops:
  0.6 103.8 %shard_map.118 = (f32[1,1]{1,0:T(1,128)}, bf16[4,2,1024]{2,1,0:T(2,128)(2,1)}, bf16[500,1024]{1,0:T(8,128)(2,1)}, f32[1,1024]{1,0:T(1,128)}, bf16[16,448]{1,0:T(8,128)(2,1)}, /*index=5*/bf16[448,1024]{1,0:T(8,128)(2,1)}) custom-call(bf16[4,2,1024]{2,1,0:T(2,128)(2,1)} %hid_ref.1, f32[1,1024]{1,0:T(1,128)} %bitcast.7, bf16[500,1024]{1,0:T(8,128)(2,1)} %bitcast.6, ...), custom_call_target="tpu_custom_call" | custom-call | tf_op jit(solution)/shard_map/pallas_call | solution.py:573
  104.4 62.0 %shard_map.119 = (f32[1,1]{1,0:T(1,128)}, bf16[4,2,1024]{2,1,0:T(2,128)(2,1)}, bf16[500,1024]{1,0:T(8,128)(2,1)}, f32[1,1024]{1,0:T(1,128)}, bf16[16,448]{1,0:T(8,128)(2,1)}, /*index=5*/bf16[448,1024]{1,0:T(8,128)(2,1)}) custom-call(f32[1,1]{1,0:T(1,128)} %get-tuple-element.18.refs_0_, bf16[4,2,1024]{2,1,0:T(2,128)(2,1)} %get-tuple-element.19.refs_1_, ...), custom_call_target="tpu_custom_call" | custom-call | tf_op jit(solution)/shard_map/pallas_call | solution.py:526

commit v3 on v2

--- a/solution.py
+++ b/solution.py
@@ -66,9 +66,9 @@
     hid_ref, gain_ref, head_ref, tgt_ref, si_ref, act_ref, dw_ref,
     loss_ref, gh_ref, ghead_ref, ggain_ref, gact_ref, gdown_ref,
     hown, ga, act, headv, headp, dwv, gheadv, gdownv, hr, hg, lg, rb, st1, st2, df, rowv,
-    po, pm, rc, d1, d2, rd1, rd2, d1b, d2b, rd1b, rd2b, ghs, erow, e1, gg1, gg2, lry, lr, fp, rf,
+    po, pm, rc, d1, d2, rd1, rd2, d1b, d2b, rd1b, rd2b, ghs, q1, rq1, rq2, gg1, gg2, ls, lr, fp, rf, gactv,
     s_act, s_in, s_out, r_a, s_a0z, s_a0y, s_a1y, s_a1z, s_ac, s_b, s_s1, s_s2, s_c, s_dc, s_d1, s_d2, s_d3, s_d4,
-    s_e1, s_g1, s_e2, s_g2, s_ec, s_f,
+    s_q1, s_q2, s_e, s_g1, s_g2, s_ec, s_f,
 ):
     width_part = hid_ref.shape[2]
     width = width_part * nv
@@ -124,7 +124,6 @@
 
     pl.semaphore_wait(barrier, ny + ng + nv - 3)
 
-    half_of = lambda p, core: lr.at[p, :, pl.ds(pl.multiple_of(core * half, half), half)]
     at_v = lambda p: df.at[pl.ds(pl.multiple_of(p * rv, rv), rv)]
     in_y = functools.partial(Exchange, ny, y, dev_y)
     in_z = functools.partial(Exchange, nz, z, dev_z)
@@ -139,10 +138,11 @@
     x_d2 = in_z(lambda p: d2.at[p], lambda p: rd2.at[p], s_d2)
     x_d3 = in_z(lambda p: d1b.at[p], lambda p: rd1b.at[p], s_d3)
     x_d4 = in_y(lambda p: d2b.at[p], lambda p: rd2b.at[p], s_d4)
-    x_e1 = in_g(lambda p: e1.at[g], lambda p: e1.at[p], s_e1)
-    x_g1 = in_g(lambda p: gg1.at[g], lambda p: gg1.at[p], s_g1)
-    x_e2 = in_y(lambda p: half_of(y, c), lambda p: half_of(p, c), s_e2)
-    x_g2 = in_y(lambda p: gg2.at[y], lambda p: gg2.at[p], s_g2)
+    x_q1 = in_y(lambda p: q1.at[p], lambda p: rq1.at[p], s_q1)
+    x_q2 = in_z(lambda p: rq2.at[z], lambda p: rq2.at[p], s_q2)
+    x_e = in_y(lambda p: ls.at[c, y], lambda p: ls.at[c, p], s_e)
+    x_g1 = in_y(lambda p: gg1.at[y], lambda p: gg1.at[p], s_g1)
+    x_g2 = in_g(lambda p: gg2.at[g], lambda p: gg2.at[p], s_g2)
     x_f = in_v(lambda p: fp.at[p], lambda p: rf.at[p], s_f)
 
     def block(dev, p, h, yy, zz, send):
@@ -347,10 +347,21 @@
     loss_ref[...] = jnp.sum(pull(6), axis=0, keepdims=True) / rows
     core_d.wait_recv()
 
-    def pack1(k, _):
+    wk = width_part // 8
+
+    def pack0(k, _):
         both = pm[k] + rc[k]
         pm[k] = both
-        d1[k] = both[:, :half].astype(BF16)
+        last = [both[zz * 8 + 6 : zz * 8 + 8] for zz in range(nz)]
+        q1[k] = stack(jnp.concatenate(last, axis=0)).astype(BF16)
+        return 0
+
+    lax.fori_loop(0, ny, pack0, 0)
+    x_q1.start()
+    rq1[y] = q1[y]
+
+    def pack1(k, _):
+        d1[k] = pm[k, :, :half].astype(BF16)
         return 0
 
     lax.fori_loop(0, ny, pack1, 0)
@@ -369,12 +380,46 @@
     x_d2.start()
     rd2[z] = d2[z]
 
-    def norm(k, _):
+    x_q1.recv()
+    line = rq1[0].astype(F32)
+    for p in range(1, ny):
+        line = line + rq1[p].astype(F32)
+    rq2[z] = line
+    x_q2.start()
+
+    def norm(k, total):
         at = pl.ds(pl.multiple_of(k * rv, rv), rv)
         hg[at, :] = (hr[at, :].astype(F32) * rowv[at, 0:1] * gain_ref[...]).astype(BF16)
-        return 0
-
-    lax.fori_loop(0, ny, norm, 0)
+        mine = pl.ds(pl.multiple_of(k * rv + c * rh, rh), rh)
+        return total + jnp.sum(pm[k] * hr[mine, :].astype(F32) * rowv[mine, 0:1], axis=0, keepdims=True)
+
+    gain_part = lax.fori_loop(0, ny, norm, jnp.zeros((1, width_part), F32))
+    for k in range(8):
+        gg1[y, k : k + 1, :] = gain_part[:, k * wk : (k + 1) * wk]
+    x_g1.start()
+
+    mine = pl.ds(pl.multiple_of(y * rv + c * rh, rh), rh)
+    of_last = lambda x: jnp.concatenate([x[zz * 8 + 6 : zz * 8 + 8] for zz in range(nz)], axis=0)
+    h_last = of_last(hr[mine, :].astype(F32))
+    scale_last = of_last(rowv[mine, 0:1])
+    inner_last = of_last(rowv[mine, 1:2])
+    x_q2.recv()
+    line = rq2[0]
+    for p in range(1, nz):
+        line = line + rq2[p]
+    grad_last = jnp.concatenate([line[: 2 * nz], line[2 * nz :]], axis=1)
+    rows_last = scale_last * (grad_last * gain_ref[...]) - h_last * (
+        scale_last * scale_last * inner_last / width
+    )
+    ls[c, y] = stack(rows_last).astype(BF16)
+
+    def pass_on(p):
+        ref = ls.at[c, p]
+        return to_core(ref, ref, s_ec.at[0, p], s_ec.at[1, p])
+
+    x_e.start()
+    pass_on(y).start()
+
     wt = min(width_part, 256)
     for m in range(0, width_part, wt):
         part = lax.dot_general(
@@ -383,6 +428,16 @@
         gheadv[:, m : m + wt] = part[:vc].astype(BF16)
     store_head = pltpu.make_async_copy(gheadv, ghead_ref, s_out.at[0])
     store_head.start()
+    x_act.recv()
+
+    def acts_in(p, _):
+        tile = act[p].astype(F32)
+        parts = [tile[zz * 4 + cc * 2 : zz * 4 + cc * 2 + 2] for cc in range(2) for zz in range(nz)]
+        act[p] = jnp.concatenate(parts, axis=0).astype(BF16)
+        return 0
+
+    x_act.sent()
+    lax.fori_loop(0, nv, acts_in, 0)
 
     x_d1.recv()
     sum1 = rd1[0].astype(F32)
@@ -400,60 +455,25 @@
         d2b[k] = stack(sum2[k * 8 : k * 8 + 8]).astype(BF16)
     x_d4.start()
     rd2b[y] = d2b[y]
-    x_d3.recv()
-    g1 = rd1b[0].astype(F32)
-    for p in range(1, nz):
-        g1 = g1 + rd1b[p].astype(F32)
-    x_d4.recv()
-    g2 = rd2b[0].astype(F32)
-    for p in range(1, ny):
-        g2 = g2 + rd2b[p].astype(F32)
-    grad_own = jnp.concatenate([g1[:8], g1[8:], g2[:8], g2[8:]], axis=1)
-
-    own_at = pl.ds(pl.multiple_of(y * rv + c * rh + z * 8, 8), 8)
-    scale_own = rowv[own_at, 0:1]
-    inner_own = rowv[own_at, 1:2]
-    h_own = hown[...]
-    grad_hid = scale_own * (grad_own * gain_ref[...]) - h_own * (scale_own * scale_own * inner_own / width)
-    ghs[...] = grad_hid
-    wk = width_part // 8
-    for k in range(8):
-        erow[2 * k : 2 * k + 2, :] = ghs[6:8, k * wk : (k + 1) * wk]
-    e1[g] = erow[...].astype(BF16)
-    x_e1.start()
-    gain_part = jnp.sum(grad_own * h_own * scale_own, axis=0, keepdims=True)
-    for k in range(8):
-        gg1[g, k : k + 1, :] = gain_part[:, k * wk : (k + 1) * wk]
-    x_g1.start()
-    for e in range(EXITS):
-        gh_ref[e] = ghs[2 * e : 2 * e + 2, :].astype(BF16)
-
-    x_e1.recv()
-    for p in range(ng):
-        tile = e1[p].astype(F32)
-        for k in range(8):
-            lry[2 * p : 2 * p + 2, k * wk : (k + 1) * wk] = tile[2 * k : 2 * k + 2]
-    lr[y] = lry[...].astype(BF16)
-    x_e2.start()
     x_g1.recv()
     gain_y = gg1[0]
-    for p in range(1, ng):
+    for p in range(1, ny):
         gain_y = gain_y + gg1[p]
-    gg2[y] = gain_y
+    gg2[g] = gain_y
     x_g2.start()
 
-    def forward_e(p):
-        to_core(half_of(p, c), half_of(p, c), s_ec.at[0, p], s_ec.at[1, p]).start()
-
-    x_e2.recv(forward_e)
-    x_act.recv()
-
-    def core_in_e(j, _):
-        p = lax.rem(y + j, ny)
-        to_core(half_of(p, o), half_of(p, o), s_ec.at[0, p], s_ec.at[1, p]).wait_recv()
+    x_e.recv(lambda p: pass_on(p).start())
+
+    def rows_out(j, _):
+        p = nearest(j)
+        ref = ls.at[o, p]
+        to_core(ref, ref, s_ec.at[0, p], s_ec.at[1, p]).wait_recv()
+        a, b = ls[0, p].astype(F32), ls[1, p].astype(F32)
+        lr[p, :, :half] = jnp.concatenate([a[: 2 * nz], b[: 2 * nz]], axis=0).astype(BF16)
+        lr[p, :, half:] = jnp.concatenate([a[2 * nz :], b[2 * nz :]], axis=0).astype(BF16)
         return 0
 
-    lax.fori_loop(1, ny, core_in_e, 0)
+    lax.fori_loop(0, ny, rows_out, 0)
     tokens = ny * lr.shape[1]
     last = lr[...].reshape(tokens, width_part)
     load_down.wait()
@@ -468,31 +488,48 @@
     gdownv[...] = down[:ff].astype(BF16)
     store_down = pltpu.make_async_copy(gdownv, gdown_ref, s_out.at[1])
     store_down.start()
+
+    x_d3.recv()
+    g1 = rd1b[0].astype(F32)
+    for p in range(1, nz):
+        g1 = g1 + rd1b[p].astype(F32)
+    x_d4.recv()
+    g2 = rd2b[0].astype(F32)
+    for p in range(1, ny):
+        g2 = g2 + rd2b[p].astype(F32)
+    grad_own = jnp.concatenate([g1[:8], g1[8:], g2[:8], g2[8:]], axis=1)
+    own_at = pl.ds(pl.multiple_of(y * rv + c * rh + z * 8, 8), 8)
+    scale_own = rowv[own_at, 0:1]
+    inner_own = rowv[own_at, 1:2]
+    ghs[...] = scale_own * (grad_own * gain_ref[...]) - hown[...] * (
+        scale_own * scale_own * inner_own / width
+    )
+    for e in range(EXITS):
+        gh_ref[e] = ghs[2 * e : 2 * e + 2, :].astype(BF16)
     x_g2.recv()
     gain_all = gg2[0]
-    for p in range(1, ny):
+    for p in range(1, ng):
         gain_all = gain_all + gg2[p]
     for k in range(8):
         ggain_ref[:, k * wk : (k + 1) * wk] = gain_all[k : k + 1, :]
+
     x_f.recv()
     acc = rf[0]
     for p in range(1, nv):
         acc = acc + rf[p]
-    gact_ref[...] = acc.astype(BF16)
+    for zz in range(nz):
+        for cc in range(2):
+            to = zz * 4 + cc * 2
+            at = cc * 2 * nz + zz * 2
+            gactv[to : to + 2, :] = acc[at : at + 2]
+    gact_ref[...] = gactv[...].astype(BF16)
 
     each(nz, z, finish(own_z))
     each(ny, y, finish(own_y))
     lax.fori_loop(0, nz, lambda zz, _: (each(ny, y, finish(on_y(zz))), 0)[1], 0)
     lax.fori_loop(0, ny, lambda yy, _: (each(nz, z, finish(on_z(yy))), 0)[1], 0)
     lax.fori_loop(0, ny, lambda yy, _: (across(yy).wait_send(), 0)[1], 0)
-    x_act.sent()
-
-    def core_out_e(j, _):
-        p = lax.rem(y + j, ny)
-        to_core(half_of(p, c), half_of(p, c), s_ec.at[0, p], s_ec.at[1, p]).wait_send()
-        return 0
-
-    lax.fori_loop(1, ny, core_out_e, 0)
+    lax.fori_loop(0, ny, lambda p, _: (pass_on(p).wait_send(), 0)[1], 0)
     each(nv, v, lambda p, _: to_tokens(p).wait_send())
     x_s1.sent()
     x_s2.sent()
@@ -502,9 +539,10 @@
     x_d2.sent()
     x_d3.sent()
     x_d4.sent()
-    x_e1.sent()
+    x_q1.sent()
+    x_q2.sent()
     x_g1.sent()
-    x_e2.sent()
+    x_e.sent()
     x_g2.sent()
     x_f.sent()
     store_head.wait()
@@ -512,11 +550,15 @@
 
 
 def hand_on_kernel(n, *refs):
-    sems = refs[2 * n]
-    copies = [pltpu.make_async_copy(refs[i], refs[n + i], sems.at[i]) for i in range(n)]
-    for copy in copies:
+    ins, outs, held, sems = refs[:n], refs[n : 2 * n], refs[2 * n : 3 * n], refs[3 * n]
+    load = [pltpu.make_async_copy(ins[i], held[i], sems.at[0, i]) for i in range(n)]
+    store = [pltpu.make_async_copy(held[i], outs[i], sems.at[1, i]) for i in range(n)]
+    for copy in load:
         copy.start()
-    for copy in copies:
+    for i in range(n):
+        load[i].wait()
+        store[i].start()
+    for copy in store:
         copy.wait()
 
 
@@ -528,7 +570,7 @@
         out_shape=tuple(jax.ShapeDtypeStruct(a.shape, a.dtype) for a in arrays),
         in_specs=[hbm] * n,
         out_specs=(hbm,) * n,
-        scratch_shapes=[pltpu.SemaphoreType.DMA((n,))],
+        scratch_shapes=[pltpu.VMEM(a.shape, a.dtype) for a in arrays] + [pltpu.SemaphoreType.DMA((2, n))],
         compiler_params=pltpu.CompilerParams(vmem_limit_bytes=56 * 1024 * 1024),
     )(*arrays)
 
@@ -558,14 +600,14 @@
         vm((ny, rh, half), BF16), vm((nz, ny * 8, half), BF16),
         vm((ny, rh, half), BF16), vm((nz, ny * 8, half), BF16),
         vm((nz, 16, q), BF16), vm((ny, 16, q), BF16), vm((nz, 16, q), BF16), vm((ny, 16, q), BF16),
-        vm((OWN, w), F32), vm((16, wk), F32), vm((ng, 16, wk), BF16),
-        vm((ng, 8, wk), F32), vm((ny, 8, wk), F32),
-        vm((tok_y, w), F32), vm((ny, tok_y, w), BF16),
-        vm((nv, tok_v, ff), F32), vm((nv, tok_v, ff), F32),
+        vm((OWN, w), F32), vm((ny, 4 * nz, half), BF16), vm((ny, 4 * nz, half), BF16), vm((nz, 4 * nz, half), F32),
+        vm((ny, 8, wk), F32), vm((ng, 8, wk), F32),
+        vm((2, ny, 4 * nz, half), BF16), vm((ny, tok_y, w), BF16),
+        vm((nv, tok_v, ff), F32), vm((nv, tok_v, ff), F32), vm((tok_v, ff), F32),
         dma(nv), sem(2), sem(2), sem(2, ny, nz), sem(nz), sem(nz, ny), sem(ny), sem(ny, nz), dma(ny),
         dma(nv), dma(ng), dma(ny), dma(nv),
         sem(2), dma(ny), dma(nz), dma(nz), dma(ny),
-        dma(ng), dma(ng), dma(ny), dma(ny), dma(ny), dma(nv),
+        dma(ny), dma(nz), dma(ny), dma(ny), dma(ng), dma(ny), dma(nv),
     ]
     spec = pl.BlockSpec(memory_space=vm)
     hbm = pl.BlockSpec(memory_space=pl.ANY)

time: 167 us -> 100 us (0.60)
  Pallas kernels: 166 us -> 99.1 us
    pallas_call x1, Pallas kernels: 62 us -> 3.29 us  [hand_on(): pl.pallas_call(functools.partial(hand_on_kernel, n), out_shape=tuple((jax...]
    pallas_call x1, Pallas kernels: 104 us -> 95.8 us  [body(): pl.pallas_call(functools.partial(kernel, ny, nz, nv, vc), out_shape=(sds(...]
where the time goes in v3:
time: 100 us; the launch traced here: 99.7 us
  Pallas kernels  99.1 us (99%)
    pallas_call x1, Pallas kernels, body(): pl.pallas_call(functools.partial(kernel, ny, nz, nv, vc), out_shape=(sds(...  95.8 us
    pallas_call x1, Pallas kernels, hand_on(): pl.pallas_call(functools.partial(hand_on_kernel, n), out_shape=tuple((jax...  3.29 us

profile of v3, /device:TPU:1, one launch (start us, length us, event | category | flops | bytes accessed | tf_op | source)
XLA Modules:
  0.0 99.7 jit_solution(14415273746361386796)
XLA Ops:
  0.6 95.8 %shard_map.118 = (f32[1,1]{1,0:T(1,128)}, bf16[4,2,1024]{2,1,0:T(2,128)(2,1)}, bf16[500,1024]{1,0:T(8,128)(2,1)}, f32[1,1024]{1,0:T(1,128)}, bf16[16,448]{1,0:T(8,128)(2,1)}, /*index=5*/bf16[448,1024]{1,0:T(8,128)(2,1)}) custom-call(bf16[4,2,1024]{2,1,0:T(2,128)(2,1)} %hid_ref.1, f32[1,1024]{1,0:T(1,128)} %bitcast.7, bf16[500,1024]{1,0:T(8,128)(2,1)} %bitcast.6, ...), custom_call_target="tpu_custom_call" | custom-call | tf_op jit(solution)/shard_map/pallas_call | solution.py:615
  96.4 3.3 %shard_map.119 = (f32[1,1]{1,0:T(1,128)}, bf16[4,2,1024]{2,1,0:T(2,128)(2,1)}, bf16[500,1024]{1,0:T(8,128)(2,1)}, f32[1,1024]{1,0:T(1,128)}, bf16[16,448]{1,0:T(8,128)(2,1)}, /*index=5*/bf16[448,1024]{1,0:T(8,128)(2,1)}) custom-call(f32[1,1]{1,0:T(1,128)} %get-tuple-element.18.refs_0_, bf16[4,2,1024]{2,1,0:T(2,128)(2,1)} %get-tuple-element.19.refs_1_, ...), custom_call_target="tpu_custom_call" | custom-call | tf_op jit(solution)/shard_map/pallas_call | solution.py:568

commit v4 on v3

--- a/solution.py
+++ b/solution.py
@@ -13,6 +13,7 @@
 BF16 = jnp.bfloat16
 EXITS = 4
 OWN = 8
+FULL = 32700.0
 VP = 512
 
 
@@ -54,6 +55,26 @@
     rest = x - hi
     mid = rest.astype(BF16).astype(F32)
     return hi, mid, rest - mid
+
+
+def to_fixed(x, extra, lanes, vc):
+    top = jnp.maximum(jnp.max(jnp.abs(x), axis=1, keepdims=True), 1e-30)
+    power = jnp.ceil(jnp.log2(top))
+    out = jnp.floor(x * (jnp.exp2(-power) * FULL) + 0.5)
+    first = jnp.floor(extra * 0.5)
+    rest = (extra * 0.5 - first) * 32768.0
+    second = jnp.floor(rest)
+    third = jnp.floor((rest - second) * 32768.0)
+    for i, value in enumerate((power, first, second, third)):
+        out = jnp.where(lanes == vc + i, value, out)
+    return out.astype(jnp.int32).astype(jnp.int16)
+
+
+def from_fixed(q, vc):
+    x = q.astype(jnp.int32).astype(F32)
+    at = lambda i: x[:, vc + i : vc + i + 1]
+    extra = 2.0 * (at(1) + (at(2) + at(3) * 2.0**-15) * 2.0**-15)
+    return x * (jnp.exp2(at(0)) * (1.0 / FULL)), extra
 
 
 def stack(x):
@@ -240,7 +261,7 @@
         part = lax.dot_general(
             hg[at, :], headp[...], (((1,), (1,)), ((), ())), preferred_element_type=F32
         )
-        lg[k] = jnp.where(lanes == vc, jnp.concatenate(sums, axis=0), part)
+        lg[k] = to_fixed(part, jnp.concatenate(sums, axis=0), lanes, vc)
 
         @pl.when(k != v)
         def _():
@@ -276,10 +297,11 @@
     valid = lanes < vc
     onehot = (column == tgt) & valid
     x_b.recv()
-    logits = rb[0]
+    logits, squares = from_fixed(rb[0], vc)
     for p in range(1, nv):
-        logits = logits + rb[p]
-    scale = lax.rsqrt(logits[:, vc : vc + 1] / width + EPS)
+        more = from_fixed(rb[p], vc)
+        logits, squares = logits + more[0], squares + more[1]
+    scale = lax.rsqrt(squares / width + EPS)
     logits = logits * scale
     peak = jnp.max(jnp.where(valid, logits, -3e38), axis=1, keepdims=True)
     grown = jnp.where(valid, jnp.exp(jnp.minimum(logits - peak, 0.0)), 0.0)
@@ -594,7 +616,7 @@
         vm((OWN, w), F32), vm((2, ny, nz, 2, 16, q), BF16),
         vm((nv, tok_v, fpad), BF16), vm((vc, w), BF16), vm((VP, w), BF16), vm((ff, w), BF16),
         vm((vc, w), BF16), vm((ff, w), BF16), vm((rows, w), BF16), vm((rows, w), BF16),
-        vm((nv, rv, VP), F32), vm((nv, rv, VP), F32),
+        vm((nv, rv, VP), jnp.int16), vm((nv, rv, VP), jnp.int16),
         vm((ng, 8, 128), F32), vm((ny, 8, 128), F32), vm((rows, VP), BF16), vm((rows, 128), F32),
         vm((ny, rh, w), F32), vm((ny, rh, w), F32), vm((ny, rh, w), F32),
         vm((ny, rh, half), BF16), vm((nz, ny * 8, half), BF16),

time: 100 us -> 94.3 us (0.943)
  Pallas kernels: 99.1 us -> 93.3 us
    pallas_call x1, Pallas kernels: 95.8 us -> 90 us  [body(): pl.pallas_call(functools.partial(kernel, ny, nz, nv, vc), out_shape=(sds(...]
where the time goes in v4:
time: 94.3 us; the launch traced here: 94 us
  Pallas kernels  93.3 us (99%)
    pallas_call x1, Pallas kernels, body(): pl.pallas_call(functools.partial(kernel, ny, nz, nv, vc), out_shape=(sds(...  90 us
    pallas_call x1, Pallas kernels, hand_on(): pl.pallas_call(functools.partial(hand_on_kernel, n), out_shape=tuple((jax...  3.29 us

profile of v4, /device:TPU:1, one launch (start us, length us, event | category | flops | bytes accessed | tf_op | source)
XLA Modules:
  0.0 94.0 jit_solution(11762124518280414460)
XLA Ops:
  0.6 90.0 %shard_map.118 = (f32[1,1]{1,0:T(1,128)}, bf16[4,2,1024]{2,1,0:T(2,128)(2,1)}, bf16[500,1024]{1,0:T(8,128)(2,1)}, f32[1,1024]{1,0:T(1,128)}, bf16[16,448]{1,0:T(8,128)(2,1)}, /*index=5*/bf16[448,1024]{1,0:T(8,128)(2,1)}) custom-call(bf16[4,2,1024]{2,1,0:T(2,128)(2,1)} %hid_ref.1, f32[1,1024]{1,0:T(1,128)} %bitcast.7, bf16[500,1024]{1,0:T(8,128)(2,1)} %bitcast.6, ...), custom_call_target="tpu_custom_call" | custom-call | tf_op jit(solution)/shard_map/pallas_call | solution.py:637
  90.7 3.3 %shard_map.119 = (f32[1,1]{1,0:T(1,128)}, bf16[4,2,1024]{2,1,0:T(2,128)(2,1)}, bf16[500,1024]{1,0:T(8,128)(2,1)}, f32[1,1024]{1,0:T(1,128)}, bf16[16,448]{1,0:T(8,128)(2,1)}, /*index=5*/bf16[448,1024]{1,0:T(8,128)(2,1)}) custom-call(f32[1,1]{1,0:T(1,128)} %get-tuple-element.18.refs_0_, bf16[4,2,1024]{2,1,0:T(2,128)(2,1)} %get-tuple-element.19.refs_1_, ...), custom_call_target="tpu_custom_call" | custom-call | tf_op jit(solution)/shard_map/pallas_call | solution.py:590

commit v5 on v4

--- a/solution.py
+++ b/solution.py
@@ -86,9 +86,9 @@
     ny, nz, nv, vc,
     hid_ref, gain_ref, head_ref, tgt_ref, si_ref, act_ref, dw_ref,
     loss_ref, gh_ref, ghead_ref, ggain_ref, gact_ref, gdown_ref,
-    hown, ga, act, headv, headp, dwv, gheadv, gdownv, hr, hg, lg, rb, st1, st2, df, rowv,
+    hown, ga, act, headv, headp, dwv, gheadv, gdownv, hr, hg, lg, rb, st1, st2, st3, ef, df, rowv,
     po, pm, rc, d1, d2, rd1, rd2, d1b, d2b, rd1b, rd2b, ghs, q1, rq1, rq2, gg1, gg2, ls, lr, fp, rf, gactv,
-    s_act, s_in, s_out, r_a, s_a0z, s_a0y, s_a1y, s_a1z, s_ac, s_b, s_s1, s_s2, s_c, s_dc, s_d1, s_d2, s_d3, s_d4,
+    s_act, s_in, s_out, r_a, s_a0z, s_a0y, s_a1y, s_a1z, s_ac, s_b, s_s1, s_s2, s_s3, s_c, s_dc, s_d1, s_d2, s_d3, s_d4,
     s_q1, s_q2, s_e, s_g1, s_g2, s_ec, s_f,
 ):
     width_part = hid_ref.shape[2]
@@ -129,7 +129,7 @@
         lax.fori_loop(1, n, one, 0)
 
     load_head = pltpu.make_async_copy(head_ref, headv, s_in.at[0])
-    load_down = pltpu.make_async_copy(dw_ref, dwv, s_in.at[1])
+    load_down = pltpu.make_async_copy(dw_ref, dwv.at[pl.ds(0, ff)], s_in.at[1])
     greet(ny, y, dev_y)
     greet(ng, g, dev_g)
     greet(nv, v, dev_v)
@@ -141,11 +141,12 @@
     ga[c, y, z, 0] = stack(hown[:, :half]).astype(BF16)
     ga[c, y, z, 1] = stack(hown[:, half:]).astype(BF16)
     act[v, :, :ff] = act_ref[...]
+    dwv[ff:, :] = jnp.zeros((dwv.shape[0] - ff, width_part), BF16)
     act[v, :, ff:] = jnp.zeros((act.shape[1], act.shape[2] - ff), BF16)
 
     pl.semaphore_wait(barrier, ny + ng + nv - 3)
 
-    at_v = lambda p: df.at[pl.ds(pl.multiple_of(p * rv, rv), rv)]
+    at_v = lambda p: ef.at[pl.ds(pl.multiple_of(p * rv, rv), rv)]
     in_y = functools.partial(Exchange, ny, y, dev_y)
     in_z = functools.partial(Exchange, nz, z, dev_z)
     in_g = functools.partial(Exchange, ng, g, dev_g)
@@ -154,6 +155,7 @@
     x_b = in_v(lambda p: lg.at[p], lambda p: rb.at[p], s_b)
     x_s1 = in_g(lambda p: st1.at[g], lambda p: st1.at[p], s_s1)
     x_s2 = in_y(lambda p: st2.at[y], lambda p: st2.at[p], s_s2)
+    x_s3 = in_v(lambda p: st3.at[v], lambda p: st3.at[p], s_s3)
     x_c = in_v(lambda p: at_v(v), at_v, s_c)
     x_d1 = in_y(lambda p: d1.at[p], lambda p: rd1.at[p], s_d1)
     x_d2 = in_z(lambda p: d2.at[p], lambda p: rd2.at[p], s_d2)
@@ -332,42 +334,64 @@
 
     put(st1, g, [to_row(peak), to_row(total), to_row(moment), to_row(picked)])
     x_s1.start()
+    out = jnp.where(onehot, 0.0, grown)
+    for i, value in enumerate(split3(peak)):
+        out = jnp.where(lanes == vc + i, value, out)
+    ef[pl.ds(pl.multiple_of(v * rv, rv), rv), :] = out.astype(BF16)
+    x_c.start()
+    weight_row, scale_row, tgt_row = to_row(weight), to_row(scale), to_row(tgt)
     x_s1.recv()
     put(st2, y, merge(st1, ng))
     x_s2.start()
     x_s2.recv()
     top, tot, mom, pick = merge(st2, ny)
-    lse = to_col(top + jnp.log(tot))
-    picked = to_col(pick)
-    inner = weight * (to_col(mom / tot) - picked)
-    dlog = weight * (jnp.exp(jnp.minimum(logits - lse, 0.0)) - onehot.astype(F32))
-    out = jnp.where(valid, dlog, 0.0)
-    for i, value in enumerate(split3(scale) + split3(inner) + split3(weight * (lse - picked))):
-        out = jnp.where(lanes == vc + i, value, out)
-    mine = pl.ds(pl.multiple_of(v * rv, rv), rv)
-    df[mine, :] = out.astype(BF16)
-
-    x_c.start()
+    lse = top + jnp.log(tot)
+    inner = weight_row * (mom / tot - pick)
+    missed = weight_row * (jnp.exp(jnp.minimum(pick - lse, 0.0)) - 1.0)
+    put(st3, v, [scale_row, inner, lse, missed, weight_row * (lse - pick), weight_row, tgt_row])
+    x_s3.start()
+    x_s3.recv()
     x_c.recv()
 
-    def rows_of(core):
+    def logit_grads(k, loss):
+        at = pl.ds(pl.multiple_of(k * rv, rv), rv)
+        scale_k, inner_k, lse_k, missed_k, _, weight_k, tgt_k = (to_col(st3[k, i : i + 1, :]) for i in range(7))
+        grown_k = ef[at, :].astype(F32)
+        peak_k = grown_k[:, vc : vc + 1] + grown_k[:, vc + 1 : vc + 2] + grown_k[:, vc + 2 : vc + 3]
+        prob = (weight_k * jnp.exp(jnp.minimum(peak_k - lse_k, 0.0))) * grown_k
+        df[at, :] = jnp.where(valid, jnp.where(column == tgt_k, missed_k, prob), 0.0).astype(BF16)
+        rowv[at, 0:1] = scale_k
+        rowv[at, 1:2] = inner_k
+        return loss + st3[k, 4:5, :]
+
+    loss = lax.fori_loop(0, nv, logit_grads, jnp.zeros((1, 128), F32))
+    in_use = lax.broadcasted_iota(jnp.int32, (1, 128), 1) < rv
+    loss_ref[...] = jnp.sum(jnp.where(in_use, loss, 0.0), axis=1, keepdims=True) / rows
+
+    hy = ny // 2
+
+    def rows_of(core, i):
         lhs = jnp.concatenate(
-            [df[pl.ds(pl.multiple_of(k * rv + core * rh, rh), rh), :] for k in range(ny)], axis=0
+            [
+                df[pl.ds(pl.multiple_of(k * rv + core * rh, rh), rh), :]
+                for k in range(i * hy, (i + 1) * hy)
+            ],
+            axis=0,
         )
-        return lax.dot_general(lhs, headp[...], (((1,), (0,)), ((), ())), preferred_element_type=F32)
-
-    po[...] = rows_of(o).reshape(ny, rh, width_part)
-    core_d = to_core(po, rc, s_dc.at[0], s_dc.at[1])
-    core_d.start()
-    pm[...] = rows_of(c).reshape(ny, rh, width_part)
-    extra = df[:, vc - vc % 128 :].astype(F32)
-    i0 = vc % 128
-    pull = lambda i: extra[:, i0 + i : i0 + i + 1] + extra[:, i0 + i + 1 : i0 + i + 2] + extra[:, i0 + i + 2 : i0 + i + 3]
-    scale_all = pull(0)
-    rowv[:, 0:1] = scale_all
-    rowv[:, 1:2] = pull(3)
-    loss_ref[...] = jnp.sum(pull(6), axis=0, keepdims=True) / rows
-    core_d.wait_recv()
+        out = lax.dot_general(lhs, headp[...], (((1,), (0,)), ((), ())), preferred_element_type=F32)
+        return out.reshape(hy, rh, width_part)
+
+    def to_other(i):
+        at = pl.ds(i * hy, hy)
+        return to_core(po.at[at], rc.at[at], s_dc.at[0, i], s_dc.at[1, i])
+
+    for i in range(2):
+        po[i * hy : (i + 1) * hy] = rows_of(o, i)
+        to_other(i).start()
+    for i in range(2):
+        pm[i * hy : (i + 1) * hy] = rows_of(c, i)
+    for i in range(2):
+        to_other(i).wait_recv()
 
     wk = width_part // 8
 
@@ -501,8 +525,9 @@
     load_down.wait()
     part = lax.dot_general(last, dwv[...], (((1,), (1,)), ((), ())), preferred_element_type=F32)
     tv = tokens // nv
+    lanes_f = lax.broadcasted_iota(jnp.int32, (tv, fp.shape[2]), 1)
     for p in range(nv):
-        fp[p] = part[p * tv : (p + 1) * tv]
+        fp[p] = to_fixed(part[p * tv : (p + 1) * tv], jnp.zeros((tv, 1), F32), lanes_f, ff)
     x_f.start()
     rf[v] = fp[v]
     acts = act[...].reshape(tokens, act.shape[2])
@@ -536,14 +561,14 @@
         ggain_ref[:, k * wk : (k + 1) * wk] = gain_all[k : k + 1, :]
 
     x_f.recv()
-    acc = rf[0]
+    acc = from_fixed(rf[0], ff)[0]
     for p in range(1, nv):
-        acc = acc + rf[p]
+        acc = acc + from_fixed(rf[p], ff)[0]
     for zz in range(nz):
         for cc in range(2):
             to = zz * 4 + cc * 2
             at = cc * 2 * nz + zz * 2
-            gactv[to : to + 2, :] = acc[at : at + 2]
+            gactv[to : to + 2, :] = acc[at : at + 2, :ff]
     gact_ref[...] = gactv[...].astype(BF16)
 
     each(nz, z, finish(own_z))
@@ -555,8 +580,10 @@
     each(nv, v, lambda p, _: to_tokens(p).wait_send())
     x_s1.sent()
     x_s2.sent()
+    x_s3.sent()
     x_c.sent()
-    core_d.wait_send()
+    for i in range(2):
+        to_other(i).wait_send()
     x_d1.sent()
     x_d2.sent()
     x_d3.sent()
@@ -614,10 +641,11 @@
     dma = lambda n: sem(2, n)
     scratch = [
         vm((OWN, w), F32), vm((2, ny, nz, 2, 16, q), BF16),
-        vm((nv, tok_v, fpad), BF16), vm((vc, w), BF16), vm((VP, w), BF16), vm((ff, w), BF16),
+        vm((nv, tok_v, fpad), BF16), vm((vc, w), BF16), vm((VP, w), BF16), vm((fpad, w), BF16),
         vm((vc, w), BF16), vm((ff, w), BF16), vm((rows, w), BF16), vm((rows, w), BF16),
         vm((nv, rv, VP), jnp.int16), vm((nv, rv, VP), jnp.int16),
-        vm((ng, 8, 128), F32), vm((ny, 8, 128), F32), vm((rows, VP), BF16), vm((rows, 128), F32),
+        vm((ng, 8, 128), F32), vm((ny, 8, 128), F32), vm((nv, 8, 128), F32),
+        vm((rows, VP), BF16), vm((rows, VP), BF16), vm((rows, 128), F32),
         vm((ny, rh, w), F32), vm((ny, rh, w), F32), vm((ny, rh, w), F32),
         vm((ny, rh, half), BF16), vm((nz, ny * 8, half), BF16),
         vm((ny, rh, half), BF16), vm((nz, ny * 8, half), BF16),
@@ -625,10 +653,10 @@
         vm((OWN, w), F32), vm((ny, 4 * nz, half), BF16), vm((ny, 4 * nz, half), BF16), vm((nz, 4 * nz, half), F32),
         vm((ny, 8, wk), F32), vm((ng, 8, wk), F32),
         vm((2, ny, 4 * nz, half), BF16), vm((ny, tok_y, w), BF16),
-        vm((nv, tok_v, ff), F32), vm((nv, tok_v, ff), F32), vm((tok_v, ff), F32),
+        vm((nv, tok_v, fpad), jnp.int16), vm((nv, tok_v, fpad), jnp.int16), vm((tok_v, ff), F32),
         dma(nv), sem(2), sem(2), sem(2, ny, nz), sem(nz), sem(nz, ny), sem(ny), sem(ny, nz), dma(ny),
-        dma(nv), dma(ng), dma(ny), dma(nv),
-        sem(2), dma(ny), dma(nz), dma(nz), dma(ny),
+        dma(nv), dma(ng), dma(ny), dma(nv), dma(nv),
+        dma(2), dma(ny), dma(nz), dma(nz), dma(ny),
         dma(ny), dma(nz), dma(ny), dma(ny), dma(ng), dma(ny), dma(nv),
     ]
     spec = pl.BlockSpec(memory_space=vm)

time: 94.3 us -> 94.5 us (level)
  no operation moved by 1% of the time
where the time goes in v5:
time: 94.5 us; the launch traced here: 94.2 us
  Pallas kernels  93.6 us (99%)
    pallas_call x1, Pallas kernels, body(): pl.pallas_call(functools.partial(kernel, ny, nz, nv, vc), out_shape=(sds(...  90.3 us
    pallas_call x1, Pallas kernels, hand_on(): pl.pallas_call(functools.partial(hand_on_kernel, n), out_shape=tuple((jax...  3.29 us

profile of v5, /device:TPU:1, one launch (start us, length us, event | category | flops | bytes accessed | tf_op | source)
XLA Modules:
  0.0 94.2 jit_solution(10965254269033971263)
XLA Ops:
  0.6 90.3 %shard_map.118 = (f32[1,1]{1,0:T(1,128)}, bf16[4,2,1024]{2,1,0:T(2,128)(2,1)}, bf16[500,1024]{1,0:T(8,128)(2,1)}, f32[1,1024]{1,0:T(1,128)}, bf16[16,448]{1,0:T(8,128)(2,1)}, /*index=5*/bf16[448,1024]{1,0:T(8,128)(2,1)}) custom-call(bf16[4,2,1024]{2,1,0:T(2,128)(2,1)} %hid_ref.1, f32[1,1024]{1,0:T(1,128)} %bitcast.7, bf16[500,1024]{1,0:T(8,128)(2,1)} %bitcast.6, ...), custom_call_target="tpu_custom_call" | custom-call | tf_op jit(solution)/shard_map/pallas_call | solution.py:665
  90.9 3.3 %shard_map.119 = (f32[1,1]{1,0:T(1,128)}, bf16[4,2,1024]{2,1,0:T(2,128)(2,1)}, bf16[500,1024]{1,0:T(8,128)(2,1)}, f32[1,1024]{1,0:T(1,128)}, bf16[16,448]{1,0:T(8,128)(2,1)}, /*index=5*/bf16[448,1024]{1,0:T(8,128)(2,1)}) custom-call(f32[1,1]{1,0:T(1,128)} %get-tuple-element.18.refs_0_, bf16[4,2,1024]{2,1,0:T(2,128)(2,1)} %get-tuple-element.19.refs_1_, ...), custom_call_target="tpu_custom_call" | custom-call | tf_op jit(solution)/shard_map/pallas_call | solution.py:617

commit v6 on v5

--- a/solution.py
+++ b/solution.py
@@ -86,9 +86,9 @@
     ny, nz, nv, vc,
     hid_ref, gain_ref, head_ref, tgt_ref, si_ref, act_ref, dw_ref,
     loss_ref, gh_ref, ghead_ref, ggain_ref, gact_ref, gdown_ref,
-    hown, ga, act, headv, headp, dwv, gheadv, gdownv, hr, hg, lg, rb, st1, st2, st3, ef, df, rowv,
+    hown, ga1, ga2, act, headv, headp, dwv, gheadv, gdownv, hr, hg, lg, rb, st1, st2, st3, ef, df, rowv,
     po, pm, rc, d1, d2, rd1, rd2, d1b, d2b, rd1b, rd2b, ghs, q1, rq1, rq2, gg1, gg2, ls, lr, fp, rf, gactv,
-    s_act, s_in, s_out, r_a, s_a0z, s_a0y, s_a1y, s_a1z, s_ac, s_b, s_s1, s_s2, s_s3, s_c, s_dc, s_d1, s_d2, s_d3, s_d4,
+    s_act, s_in, s_out, s_a1, s_a2, s_a3, s_a4, s_c1, s_c2, s_b, s_s1, s_s2, s_s3, s_c, s_dc, s_d1, s_d2, s_d3, s_d4,
     s_q1, s_q2, s_e, s_g1, s_g2, s_ec, s_f,
 ):
     width_part = hid_ref.shape[2]
@@ -138,8 +138,8 @@
 
     for e in range(EXITS):
         hown[2 * e : 2 * e + 2, :] = hid_ref[e].astype(F32)
-    ga[c, y, z, 0] = stack(hown[:, :half]).astype(BF16)
-    ga[c, y, z, 1] = stack(hown[:, half:]).astype(BF16)
+    ga1[c, y, z] = stack(hown[:, :half]).astype(BF16)
+    ga2[c, z, y] = stack(hown[:, half:]).astype(BF16)
     act[v, :, :ff] = act_ref[...]
     dwv[ff:, :] = jnp.zeros((dwv.shape[0] - ff, width_part), BF16)
     act[v, :, ff:] = jnp.zeros((act.shape[1], act.shape[2] - ff), BF16)
@@ -151,10 +151,14 @@
     in_z = functools.partial(Exchange, nz, z, dev_z)
     in_g = functools.partial(Exchange, ng, g, dev_g)
     in_v = functools.partial(Exchange, nv, v, dev_v)
+    x_a1 = in_z(lambda p: ga1.at[c, y, z], lambda p: ga1.at[c, y, p], s_a1)
+    x_a2 = in_y(lambda p: ga2.at[c, z, y], lambda p: ga2.at[c, z, p], s_a2)
+    x_a3 = in_y(lambda p: ga1.at[c, y], lambda p: ga1.at[c, p], s_a3)
+    x_a4 = in_z(lambda p: ga2.at[c, z], lambda p: ga2.at[c, p], s_a4)
     x_act = in_v(lambda p: act.at[v], lambda p: act.at[p], s_act)
     x_b = in_v(lambda p: lg.at[p], lambda p: rb.at[p], s_b)
-    x_s1 = in_g(lambda p: st1.at[g], lambda p: st1.at[p], s_s1)
-    x_s2 = in_y(lambda p: st2.at[y], lambda p: st2.at[p], s_s2)
+    x_s1 = in_y(lambda p: st1.at[y], lambda p: st1.at[p], s_s1)
+    x_s2 = in_g(lambda p: st2.at[g], lambda p: st2.at[p], s_s2)
     x_s3 = in_v(lambda p: st3.at[v], lambda p: st3.at[p], s_s3)
     x_c = in_v(lambda p: at_v(v), at_v, s_c)
     x_d1 = in_y(lambda p: d1.at[p], lambda p: rd1.at[p], s_d1)
@@ -168,13 +172,6 @@
     x_g2 = in_g(lambda p: gg2.at[g], lambda p: gg2.at[p], s_g2)
     x_f = in_v(lambda p: fp.at[p], lambda p: rf.at[p], s_f)
 
-    def block(dev, p, h, yy, zz, send):
-        ref = ga.at[c, yy, zz, h]
-        return pltpu.make_async_remote_copy(
-            src_ref=ref, dst_ref=ref, send_sem=send, recv_sem=r_a.at[h, yy, zz],
-            device_id=dev(p), device_id_type=MESH,
-        )
-
     def each(n, me, do):
         def one(j, _):
             do(lax.rem(me + j, n), j)
@@ -182,20 +179,20 @@
 
         lax.fori_loop(1, n, one, 0)
 
-    own_z = lambda p, j: block(dev_z, p, 0, y, z, s_a0z.at[j])
-    own_y = lambda p, j: block(dev_y, p, 1, y, z, s_a1y.at[j])
-    on_y = lambda zz: lambda p, j: block(dev_y, p, 0, y, zz, s_a0y.at[zz, j])
-    on_z = lambda yy: lambda p, j: block(dev_z, p, 1, yy, z, s_a1z.at[yy, j])
-    begin = lambda make: lambda p, j: make(p, j).start()
-    finish = lambda make: lambda p, j: make(p, j).wait_send()
-
-    def arrived(h, yy, zz):
-        block(dev_y, y, h, yy, zz, s_a0z.at[0]).wait_recv()
-
-    each(nz, z, begin(own_z))
-    each(ny, y, begin(own_y))
-    each(ny, y, begin(on_y(z)))
-    each(nz, z, begin(on_z(y)))
+    def across1(p, core):
+        return to_core(ga1.at[core, p], ga1.at[core, p], s_c1.at[0, p], s_c1.at[1, p])
+
+    def across2(p, core):
+        return to_core(ga2.at[core, p], ga2.at[core, p], s_c2.at[0, p], s_c2.at[1, p])
+
+    x_a1.start()
+    x_a2.start()
+    x_a1.recv()
+    x_a3.start()
+    x_a2.recv()
+    x_a4.start()
+    across1(y, c).start()
+    across2(z, c).start()
     x_act.start()
 
     load_head.wait()
@@ -204,34 +201,16 @@
     tail = headv[cut:vc, :].astype(F32)
     headp[cut:, :] = jnp.concatenate([tail, jnp.zeros((VP - vc, width_part), F32)], axis=0).astype(BF16)
 
-    for d in range(1, max(ny, nz) // 2 + 1):
-        for shift in (d, -d):
-            if d <= ny // 2 and (shift > 0 or 2 * d < ny):
-                yy = lax.rem(y + shift + ny, ny)
-                arrived(1, yy, z)
-                each(nz, z, begin(on_z(yy)))
-            if d <= nz // 2 and (shift > 0 or 2 * d < nz):
-                zz = lax.rem(z + shift + nz, nz)
-                arrived(0, y, zz)
-                each(ny, y, begin(on_y(zz)))
-
-    def across(yy):
-        ref = ga.at[c, yy]
-        return to_core(ref, ref, s_ac.at[0, yy], s_ac.at[1, yy])
+    x_a4.recv(lambda p: across2(p, c).start())
+    lax.fori_loop(0, nz, lambda p, _: (across2(p, o).wait_recv(), 0)[1], 0)
 
     def nearest(j):
         return lax.rem(y + ny + jnp.where(j % 2 == 1, (j + 1) // 2, -(j // 2)), ny)
 
-    def line_of(j, _):
-        yy = nearest(j)
-
-        @pl.when(j > 0)
-        def _():
-            lax.fori_loop(0, nz, lambda zz, _: (arrived(0, yy, zz), 0)[1], 0)
-
-        each(nz, z, lambda p, _: arrived(1, yy, p))
-        across(yy).start()
-        return 0
+    def line_of(j):
+        p = nearest(j)
+        x_a3.copy(p, 0, x_a3.slot(p), x_a3.slot(p), p).wait_recv()
+        across1(p, c).start()
 
     lanes = lax.broadcasted_iota(jnp.int32, (rv, VP), 1)
 
@@ -243,7 +222,7 @@
 
     def rows_in(j):
         k = nearest(j)
-        to_core(ga.at[o, k], ga.at[o, k], s_ac.at[0, k], s_ac.at[1, k]).wait_recv()
+        across1(k, o).wait_recv()
         at = pl.ds(pl.multiple_of(k * rv, rv), rv)
         sums = []
         for cc in range(2):
@@ -251,8 +230,8 @@
                 to_at = pl.ds(pl.multiple_of(k * rv + cc * rh + zz * OWN, 16), 16)
                 squares = None
                 for h in range(2):
-                    a = ga[cc, k, zz, h].astype(F32)
-                    b = ga[cc, k, zz + 1, h].astype(F32)
+                    a = (ga1[cc, k, zz] if h == 0 else ga2[cc, zz, k]).astype(F32)
+                    b = (ga1[cc, k, zz + 1] if h == 0 else ga2[cc, zz + 1, k]).astype(F32)
                     for s in range(2):
                         x = jnp.concatenate([a[s * 8 : s * 8 + 8], b[s * 8 : s * 8 + 8]], axis=0)
                         to = slice((2 * h + s) * q, (2 * h + s + 1) * q)
@@ -273,10 +252,8 @@
         def _():
             rb[v] = lg[v]
 
-    line_of(0, 0)
-
     def step(j, _):
-        line_of(j, 0)
+        line_of(j)
         rows_in(j - 1)
         return 0
 
@@ -332,7 +309,7 @@
             pick = pick + ref[p, 3:4, :]
         return top, tot, mom, pick
 
-    put(st1, g, [to_row(peak), to_row(total), to_row(moment), to_row(picked)])
+    put(st1, y, [to_row(peak), to_row(total), to_row(moment), to_row(picked)])
     x_s1.start()
     out = jnp.where(onehot, 0.0, grown)
     for i, value in enumerate(split3(peak)):
@@ -341,10 +318,10 @@
     x_c.start()
     weight_row, scale_row, tgt_row = to_row(weight), to_row(scale), to_row(tgt)
     x_s1.recv()
-    put(st2, y, merge(st1, ng))
+    put(st2, g, merge(st1, ny))
     x_s2.start()
     x_s2.recv()
-    top, tot, mom, pick = merge(st2, ny)
+    top, tot, mom, pick = merge(st2, ng)
     lse = top + jnp.log(tot)
     inner = weight_row * (mom / tot - pick)
     missed = weight_row * (jnp.exp(jnp.minimum(pick - lse, 0.0)) - 1.0)
@@ -414,6 +391,13 @@
     x_d1.start()
     rd1[y] = d1[y]
 
+    x_q1.recv()
+    line = rq1[0].astype(F32)
+    for p in range(1, ny):
+        line = line + rq1[p].astype(F32)
+    rq2[z] = line
+    x_q2.start()
+
     def pack2(k, _):
         for zz in range(nz):
             pair = jnp.concatenate(
@@ -425,13 +409,6 @@
     lax.fori_loop(0, ny // 2, pack2, 0)
     x_d2.start()
     rd2[z] = d2[z]
-
-    x_q1.recv()
-    line = rq1[0].astype(F32)
-    for p in range(1, ny):
-        line = line + rq1[p].astype(F32)
-    rq2[z] = line
-    x_q2.start()
 
     def norm(k, total):
         at = pl.ds(pl.multiple_of(k * rv, rv), rv)
@@ -571,11 +548,13 @@
             gactv[to : to + 2, :] = acc[at : at + 2, :ff]
     gact_ref[...] = gactv[...].astype(BF16)
 
-    each(nz, z, finish(own_z))
-    each(ny, y, finish(own_y))
-    lax.fori_loop(0, nz, lambda zz, _: (each(ny, y, finish(on_y(zz))), 0)[1], 0)
-    lax.fori_loop(0, ny, lambda yy, _: (each(nz, z, finish(on_z(yy))), 0)[1], 0)
-    lax.fori_loop(0, ny, lambda yy, _: (across(yy).wait_send(), 0)[1], 0)
+    x_a1.sent()
+    x_a2.sent()
+    x_a3.sent()
+    x_a4.sent()
+    lax.fori_loop(0, ny, lambda p, _: (across1(p, c).wait_send(), 0)[1], 0)
+    lax.fori_loop(0, nz, lambda p, _: (across2(p, c).wait_send(), 0)[1], 0)
+
     lax.fori_loop(0, ny, lambda p, _: (pass_on(p).wait_send(), 0)[1], 0)
     each(nv, v, lambda p, _: to_tokens(p).wait_send())
     x_s1.sent()
@@ -640,11 +619,11 @@
     sem = lambda *n: pltpu.SemaphoreType.DMA(n)
     dma = lambda n: sem(2, n)
     scratch = [
-        vm((OWN, w), F32), vm((2, ny, nz, 2, 16, q), BF16),
+        vm((OWN, w), F32), vm((2, ny, nz, 16, q), BF16), vm((2, nz, ny, 16, q), BF16),
         vm((nv, tok_v, fpad), BF16), vm((vc, w), BF16), vm((VP, w), BF16), vm((fpad, w), BF16),
         vm((vc, w), BF16), vm((ff, w), BF16), vm((rows, w), BF16), vm((rows, w), BF16),
         vm((nv, rv, VP), jnp.int16), vm((nv, rv, VP), jnp.int16),
-        vm((ng, 8, 128), F32), vm((ny, 8, 128), F32), vm((nv, 8, 128), F32),
+        vm((ny, 8, 128), F32), vm((ng, 8, 128), F32), vm((nv, 8, 128), F32),
         vm((rows, VP), BF16), vm((rows, VP), BF16), vm((rows, 128), F32),
         vm((ny, rh, w), F32), vm((ny, rh, w), F32), vm((ny, rh, w), F32),
         vm((ny, rh, half), BF16), vm((nz, ny * 8, half), BF16),
@@ -654,8 +633,8 @@
         vm((ny, 8, wk), F32), vm((ng, 8, wk), F32),
         vm((2, ny, 4 * nz, half), BF16), vm((ny, tok_y, w), BF16),
         vm((nv, tok_v, fpad), jnp.int16), vm((nv, tok_v, fpad), jnp.int16), vm((tok_v, ff), F32),
-        dma(nv), sem(2), sem(2), sem(2, ny, nz), sem(nz), sem(nz, ny), sem(ny), sem(ny, nz), dma(ny),
-        dma(nv), dma(ng), dma(ny), dma(nv), dma(nv),
+        dma(nv), sem(2), sem(2), dma(nz), dma(ny), dma(ny), dma(nz), dma(ny), dma(nz),
+        dma(nv), dma(ny), dma(ng), dma(nv), dma(nv),
         dma(2), dma(ny), dma(nz), dma(nz), dma(ny),
         dma(ny), dma(nz), dma(ny), dma(ny), dma(ng), dma(ny), dma(nv),
     ]

time: 94.5 us -> 102 us (1.079)
  Pallas kernels: 93.6 us -> 101 us
    pallas_call x1, Pallas kernels: 90.3 us -> 98 us  [body(): pl.pallas_call(functools.partial(kernel, ny, nz, nv, vc), out_shape=(sds(...]
where the time goes in v6:
time: 102 us
  Pallas kernels  101 us (99%)
    pallas_call x1, Pallas kernels, body(): pl.pallas_call(functools.partial(kernel, ny, nz, nv, vc), out_shape=(sds(...  98 us
    pallas_call x1, Pallas kernels, hand_on(): pl.pallas_call(functools.partial(hand_on_kernel, n), out_shape=tuple((jax...  3.29 us

profile of v6, /device:TPU:1, one launch (start us, length us, event | category | flops | bytes accessed | tf_op | source)
XLA Modules:
  0.0 101.9 jit_solution(5122274177228750544)
XLA Ops:
  0.6 98.0 %shard_map.118 = (f32[1,1]{1,0:T(1,128)}, bf16[4,2,1024]{2,1,0:T(2,128)(2,1)}, bf16[500,1024]{1,0:T(8,128)(2,1)}, f32[1,1024]{1,0:T(1,128)}, bf16[16,448]{1,0:T(8,128)(2,1)}, /*index=5*/bf16[448,1024]{1,0:T(8,128)(2,1)}) custom-call(bf16[4,2,1024]{2,1,0:T(2,128)(2,1)} %hid_ref.1, f32[1,1024]{1,0:T(1,128)} %bitcast.7, bf16[500,1024]{1,0:T(8,128)(2,1)} %bitcast.6, ...), custom_call_target="tpu_custom_call" | custom-call | tf_op jit(solution)/shard_map/pallas_call | solution.py:644
  98.6 3.3 %shard_map.119 = (f32[1,1]{1,0:T(1,128)}, bf16[4,2,1024]{2,1,0:T(2,128)(2,1)}, bf16[500,1024]{1,0:T(8,128)(2,1)}, f32[1,1024]{1,0:T(1,128)}, bf16[16,448]{1,0:T(8,128)(2,1)}, /*index=5*/bf16[448,1024]{1,0:T(8,128)(2,1)}) custom-call(f32[1,1]{1,0:T(1,128)} %get-tuple-element.18.refs_0_, bf16[4,2,1024]{2,1,0:T(2,128)(2,1)} %get-tuple-element.19.refs_1_, ...), custom_call_target="tpu_custom_call" | custom-call | tf_op jit(solution)/shard_map/pallas_call | solution.py:596

commit v7 on v5

--- a/solution.py
+++ b/solution.py
@@ -196,7 +196,6 @@
     each(ny, y, begin(own_y))
     each(ny, y, begin(on_y(z)))
     each(nz, z, begin(on_z(y)))
-    x_act.start()
 
     load_head.wait()
     cut = vc // 16 * 16
@@ -338,11 +337,11 @@
     for i, value in enumerate(split3(peak)):
         out = jnp.where(lanes == vc + i, value, out)
     ef[pl.ds(pl.multiple_of(v * rv, rv), rv), :] = out.astype(BF16)
-    x_c.start()
     weight_row, scale_row, tgt_row = to_row(weight), to_row(scale), to_row(tgt)
     x_s1.recv()
     put(st2, y, merge(st1, ng))
     x_s2.start()
+    x_c.start()
     x_s2.recv()
     top, tot, mom, pick = merge(st2, ny)
     lse = top + jnp.log(tot)
@@ -350,6 +349,7 @@
     missed = weight_row * (jnp.exp(jnp.minimum(pick - lse, 0.0)) - 1.0)
     put(st3, v, [scale_row, inner, lse, missed, weight_row * (lse - pick), weight_row, tgt_row])
     x_s3.start()
+    x_act.start()
     x_s3.recv()
     x_c.recv()
 
@@ -386,7 +386,7 @@
         return to_core(po.at[at], rc.at[at], s_dc.at[0, i], s_dc.at[1, i])
 
     for i in range(2):
-        po[i * hy : (i + 1) * hy] = rows_of(o, i)
+        po[i * hy : (i + 1) * hy] = rows_of(o, i).astype(BF16)
         to_other(i).start()
     for i in range(2):
         pm[i * hy : (i + 1) * hy] = rows_of(c, i)
@@ -396,7 +396,7 @@
     wk = width_part // 8
 
     def pack0(k, _):
-        both = pm[k] + rc[k]
+        both = pm[k] + rc[k].astype(F32)
         pm[k] = both
         last = [both[zz * 8 + 6 : zz * 8 + 8] for zz in range(nz)]
         q1[k] = stack(jnp.concatenate(last, axis=0)).astype(BF16)
@@ -646,7 +646,7 @@
         vm((nv, rv, VP), jnp.int16), vm((nv, rv, VP), jnp.int16),
         vm((ng, 8, 128), F32), vm((ny, 8, 128), F32), vm((nv, 8, 128), F32),
         vm((rows, VP), BF16), vm((rows, VP), BF16), vm((rows, 128), F32),
-        vm((ny, rh, w), F32), vm((ny, rh, w), F32), vm((ny, rh, w), F32),
+        vm((ny, rh, w), BF16), vm((ny, rh, w), F32), vm((ny, rh, w), BF16),
         vm((ny, rh, half), BF16), vm((nz, ny * 8, half), BF16),
         vm((ny, rh, half), BF16), vm((nz, ny * 8, half), BF16),
         vm((nz, 16, q), BF16), vm((ny, 16, q), BF16), vm((nz, 16, q), BF16), vm((ny, 16, q), BF16),

time: 94.5 us -> 92.4 us (0.978)
  Pallas kernels: 93.6 us -> 91.4 us
    pallas_call x1, Pallas kernels: 90.3 us -> 88.1 us  [body(): pl.pallas_call(functools.partial(kernel, ny, nz, nv, vc), out_shape=(sds(...]
where the time goes in v7:
time: 92.4 us; the launch traced here: 92 us
  Pallas kernels  91.4 us (99%)
    pallas_call x1, Pallas kernels, body(): pl.pallas_call(functools.partial(kernel, ny, nz, nv, vc), out_shape=(sds(...  88.1 us
    pallas_call x1, Pallas kernels, hand_on(): pl.pallas_call(functools.partial(hand_on_kernel, n), out_shape=tuple((jax...  3.29 us

profile of v7, /device:TPU:1, one launch (start us, length us, event | category | flops | bytes accessed | tf_op | source)
XLA Modules:
  0.0 92.0 jit_solution(12805048865411938150)
XLA Ops:
  0.6 88.1 %shard_map.118 = (f32[1,1]{1,0:T(1,128)}, bf16[4,2,1024]{2,1,0:T(2,128)(2,1)}, bf16[500,1024]{1,0:T(8,128)(2,1)}, f32[1,1024]{1,0:T(1,128)}, bf16[16,448]{1,0:T(8,128)(2,1)}, /*index=5*/bf16[448,1024]{1,0:T(8,128)(2,1)}) custom-call(bf16[4,2,1024]{2,1,0:T(2,128)(2,1)} %hid_ref.1, f32[1,1024]{1,0:T(1,128)} %bitcast.7, bf16[500,1024]{1,0:T(8,128)(2,1)} %bitcast.6, ...), custom_call_target="tpu_custom_call" | custom-call | tf_op jit(solution)/shard_map/pallas_call | solution.py:665
  88.8 3.3 %shard_map.119 = (f32[1,1]{1,0:T(1,128)}, bf16[4,2,1024]{2,1,0:T(2,128)(2,1)}, bf16[500,1024]{1,0:T(8,128)(2,1)}, f32[1,1024]{1,0:T(1,128)}, bf16[16,448]{1,0:T(8,128)(2,1)}, /*index=5*/bf16[448,1024]{1,0:T(8,128)(2,1)}) custom-call(f32[1,1]{1,0:T(1,128)} %get-tuple-element.18.refs_0_, bf16[4,2,1024]{2,1,0:T(2,128)(2,1)} %get-tuple-element.19.refs_1_, ...), custom_call_target="tpu_custom_call" | custom-call | tf_op jit(solution)/shard_map/pallas_call | solution.py:617

commit v8 on v7

--- a/solution.py
+++ b/solution.py
@@ -27,16 +27,15 @@
             device_id=self.dev(p), device_id_type=MESH,
         )
 
-    def each(self, do):
+    def each(self, do, lo=1, hi=None):
         def one(j, _):
             do(lax.rem(self.me + j, self.n), j)
             return 0
 
-        lax.fori_loop(1, self.n, one, 0)
-
-    def start(self):
-        self.each(lambda p, j: self.copy(p, j, self.src(p), self.slot(self.me), self.me).start())
-        return self
+        lax.fori_loop(lo, self.n if hi is None else hi, one, 0)
+
+    def start(self, lo=1, hi=None):
+        self.each(lambda p, j: self.copy(p, j, self.src(p), self.slot(self.me), self.me).start(), lo, hi)
 
     def recv(self, then=None):
         def one(p, j):
@@ -337,11 +336,12 @@
     for i, value in enumerate(split3(peak)):
         out = jnp.where(lanes == vc + i, value, out)
     ef[pl.ds(pl.multiple_of(v * rv, rv), rv), :] = out.astype(BF16)
+    x_c.start(1, nv // 2)
     weight_row, scale_row, tgt_row = to_row(weight), to_row(scale), to_row(tgt)
     x_s1.recv()
     put(st2, y, merge(st1, ng))
     x_s2.start()
-    x_c.start()
+    x_c.start(nv // 2)
     x_s2.recv()
     top, tot, mom, pick = merge(st2, ny)
     lse = top + jnp.log(tot)

time: 92.4 us -> 93.5 us (1.012)
    pallas_call x1, Pallas kernels: 88.1 us -> 89.1 us  [body(): pl.pallas_call(functools.partial(kernel, ny, nz, nv, vc), out_shape=(sds(...]
where the time goes in v8:
time: 93.5 us; the launch traced here: 93 us
  Pallas kernels  92.3 us (99%)
    pallas_call x1, Pallas kernels, body(): pl.pallas_call(functools.partial(kernel, ny, nz, nv, vc), out_shape=(sds(...  89.1 us
    pallas_call x1, Pallas kernels, hand_on(): pl.pallas_call(functools.partial(hand_on_kernel, n), out_shape=tuple((jax...  3.29 us

profile of v8, /device:TPU:1, one launch (start us, length us, event | category | flops | bytes accessed | tf_op | source)
XLA Modules:
  0.0 93.0 jit_solution(15513921525249227433)
XLA Ops:
  0.6 89.1 %shard_map.118 = (f32[1,1]{1,0:T(1,128)}, bf16[4,2,1024]{2,1,0:T(2,128)(2,1)}, bf16[500,1024]{1,0:T(8,128)(2,1)}, f32[1,1024]{1,0:T(1,128)}, bf16[16,448]{1,0:T(8,128)(2,1)}, /*index=5*/bf16[448,1024]{1,0:T(8,128)(2,1)}) custom-call(bf16[4,2,1024]{2,1,0:T(2,128)(2,1)} %hid_ref.1, f32[1,1024]{1,0:T(1,128)} %bitcast.7, bf16[500,1024]{1,0:T(8,128)(2,1)} %bitcast.6, ...), custom_call_target="tpu_custom_call" | custom-call | tf_op jit(solution)/shard_map/pallas_call | solution.py:665
  89.7 3.3 %shard_map.119 = (f32[1,1]{1,0:T(1,128)}, bf16[4,2,1024]{2,1,0:T(2,128)(2,1)}, bf16[500,1024]{1,0:T(8,128)(2,1)}, f32[1,1024]{1,0:T(1,128)}, bf16[16,448]{1,0:T(8,128)(2,1)}, /*index=5*/bf16[448,1024]{1,0:T(8,128)(2,1)}) custom-call(f32[1,1]{1,0:T(1,128)} %get-tuple-element.18.refs_0_, bf16[4,2,1024]{2,1,0:T(2,128)(2,1)} %get-tuple-element.19.refs_1_, ...), custom_call_target="tpu_custom_call" | custom-call | tf_op jit(solution)/shard_map/pallas_call | solution.py:617
